TPU v7x, 32 devices: a whole 2x2x4 slice. The times are simulated.
32 devices in a mesh: rep: 4 (over y, x), shard: 8 (over z, core).
Axes of the slice: x: 2, y: 2, z: 4, core: 2. Of those that a mesh axis runs over, the one named last changes fastest.
Arguments:
- inner_wqkv: float32 [4, 2048, 4096], P('rep', 'shard'), may hold values from -8.5 to 8.5
- inner_w1: float32 [4, 2048, 6144], P('rep', 'shard'), may hold values from -8.5 to 8.5
- inner_w3: float32 [4, 2048, 6144], P('rep', 'shard'), may hold values from -8.5 to 8.5
- inner_wo: float32 [4, 2048, 2048], P('rep', 'shard'), may hold values from -8.5 to 8.5
- inner_w2: float32 [4, 6144, 2048], P('rep', 'shard'), may hold values from -8.5 to 8.5
- outer_wqkv: float32 [2048, 4096], P('shard', 'rep'), may hold values from -8 to 8
- outer_w1: float32 [2048, 6144], P('shard', 'rep'), may hold values from -8 to 8
- outer_w3: float32 [2048, 6144], P('shard', 'rep'), may hold values from -8 to 8
- outer_wo: float32 [2048, 2048], P('shard', 'rep'), may hold values from -8 to 8
- outer_w2: float32 [6144, 2048], P('shard', 'rep'), may hold values from -8 to 8
- moment_wqkv: float32 [2048, 4096], P('shard', 'rep'), may hold values from -0.4 to 0.4
- moment_w1: float32 [2048, 6144], P('shard', 'rep'), may hold values from -0.4 to 0.4
- moment_w3: float32 [2048, 6144], P('shard', 'rep'), may hold values from -0.4 to 0.4
- moment_wo: float32 [2048, 2048], P('shard', 'rep'), may hold values from -0.4 to 0.4
- moment_w2: float32 [6144, 2048], P('shard', 'rep'), may hold values from -0.4 to 0.4
- basis_wo: float32 [2048, 64], P('shard'), may hold values from -0.5 to 0.5
- basis_w2: float32 [6144, 64], P('shard'), may hold values from -0.3125 to 0.3125
Outputs:
- weights_wqkv: bfloat16 [2048, 4096], P('shard')
- weights_w1: bfloat16 [2048, 6144], P('shard')
- weights_w3: bfloat16 [2048, 6144], P('shard')
- weights_wo: bfloat16 [2048, 2048], P('shard')
- weights_w2: bfloat16 [6144, 2048], P('shard')
- master_wqkv: float32 [2048, 4096], P('shard', 'rep')
- master_w1: float32 [2048, 6144], P('shard', 'rep')
- master_w3: float32 [2048, 6144], P('shard', 'rep')
- master_wo: float32 [2048, 2048], P('shard', 'rep')
- master_w2: float32 [6144, 2048], P('shard', 'rep')
- momentum_wqkv: float32 [2048, 4096], P('shard', 'rep')
- momentum_w1: float32 [2048, 6144], P('shard', 'rep')
- momentum_w3: float32 [2048, 6144], P('shard', 'rep')
- momentum_wo: float32 [2048, 2048], P('shard', 'rep')
- momentum_w2: float32 [6144, 2048], P('shard', 'rep')
All inputs are finite; a program needn't handle non-finite values.
Results may differ from a plain program's by a relative error of at most 0.007.
Values may be sent and summed in bfloat16 or wider, within the bound.
A program may use at most 128 MiB of HBM per device.

v0:
```python
import jax
import jax.numpy as jnp
from jax import lax
from jax.sharding import PartitionSpec as P

rate_outer = 0.7
decay_moment = 0.9


def project(basis, matrix):
    return lax.dot_general(
        basis,
        matrix,
        (((0,), (0,)), ((), ())),
        precision=lax.Precision.HIGHEST,
        preferred_element_type=jnp.float32,
    )


def rebuild(basis, coeff):
    return jnp.dot(
        basis, coeff, precision=lax.Precision.HIGHEST, preferred_element_type=jnp.float32
    )


def nesterov(outer, moment, delta):
    moment_new = decay_moment * moment + delta
    master = outer - rate_outer * (delta + decay_moment * moment_new)
    return (master.astype(jnp.bfloat16), master, moment_new)


def on_device(
    inner_wqkv,
    inner_w1,
    inner_w3,
    inner_wo,
    inner_w2,
    outer_wqkv,
    outer_w1,
    outer_w3,
    outer_wo,
    outer_w2,
    moment_wqkv,
    moment_w1,
    moment_w3,
    moment_wo,
    moment_w2,
    basis_wo,
    basis_w2,
):
    groups = lax.axis_size("rep")
    width = outer_wo.shape[1]
    start = lax.axis_index("rep") * width
    summed = (
        lax.psum_scatter(inner_wqkv[0], "rep", scatter_dimension=1, tiled=True),
        lax.psum_scatter(inner_w1[0], "rep", scatter_dimension=1, tiled=True),
        lax.psum_scatter(inner_w3[0], "rep", scatter_dimension=1, tiled=True),
    )
    d_qkv = outer_wqkv - summed[0] / groups
    d_one = outer_w1 - summed[1] / groups
    d_three = outer_w3 - summed[2] / groups
    pairs = ((inner_wo[0], outer_wo, basis_wo), (inner_w2[0], outer_w2, basis_w2))
    terms = []
    for inner_part, outer_part, basis in pairs:
        whole_proj = -project(basis, inner_part) / groups
        owned = project(basis, outer_part) + lax.dynamic_slice_in_dim(whole_proj, start, width, 1)
        terms.append(lax.dynamic_update_slice_in_dim(whole_proj, owned, start, 1))
    totals = lax.psum((terms[0], terms[1]), ("rep", "shard"))
    coeff_out = lax.dynamic_slice_in_dim(totals[0], start, width, 1)
    coeff_down = lax.dynamic_slice_in_dim(totals[1], start, width, 1)
    d_out = rebuild(basis_wo, coeff_out)
    d_down = rebuild(basis_w2, coeff_down)
    a0, b0, c0 = nesterov(outer_wqkv, moment_wqkv, d_qkv)
    a1, b1, c1 = nesterov(outer_w1, moment_w1, d_one)
    a3, b3, c3 = nesterov(outer_w3, moment_w3, d_three)
    ao, bo, co = nesterov(outer_wo, moment_wo, d_out)
    a2, b2, c2 = nesterov(outer_w2, moment_w2, d_down)
    fresh = (
        lax.all_gather(a0, "rep", axis=1, tiled=True),
        lax.all_gather(a1, "rep", axis=1, tiled=True),
        lax.all_gather(a3, "rep", axis=1, tiled=True),
        lax.all_gather(ao, "rep", axis=1, tiled=True),
        lax.all_gather(a2, "rep", axis=1, tiled=True),
    )
    return (
        fresh[0],
        fresh[1],
        fresh[2],
        fresh[3],
        fresh[4],
        b0,
        b1,
        b3,
        bo,
        b2,
        c0,
        c1,
        c3,
        co,
        c2,
    )


def solution(mesh):
    return jax.shard_map(
        on_device,
        mesh=mesh,
        in_specs=(
            P("rep", "shard", None),
            P("rep", "shard", None),
            P("rep", "shard", None),
            P("rep", "shard", None),
            P("rep", "shard", None),
            P("shard", "rep"),
            P("shard", "rep"),
            P("shard", "rep"),
            P("shard", "rep"),
            P("shard", "rep"),
            P("shard", "rep"),
            P("shard", "rep"),
            P("shard", "rep"),
            P("shard", "rep"),
            P("shard", "rep"),
            P("shard", None),
            P("shard", None),
        ),
        out_specs=(
            P("shard", None),
            P("shard", None),
            P("shard", None),
            P("shard", None),
            P("shard", None),
            P("shard", "rep"),
            P("shard", "rep"),
            P("shard", "rep"),
            P("shard", "rep"),
            P("shard", "rep"),
            P("shard", "rep"),
            P("shard", "rep"),
            P("shard", "rep"),
            P("shard", "rep"),
            P("shard", "rep"),
        ),
        check_vma=False,
    )
```

profile of v0, /device:TPU:0, one launch (start us, length us, event | category | flops | bytes accessed | tf_op | source)
XLA Modules:
  0.0 450.0 jit_solution(431255285296983832)
XLA Ops:
  8.0 0.0 all-reduce.3.cloned.1.call-start
  8.1 1.5 copy-done
  9.6 2.2 fusion.5
  11.9 6.1 %fusion.6 = f32[64,2048]{1,0:T(8,128)S(1)} fusion(f32[768,64]{0,1:T(8,128)S(1)} %copy-done.10, f32[1,768,2048]{2,1,0:T(8,128)} %param.21), kind=kOutput, calls=%fused_computation.5 | convolution fusion | flops 1208221696 | bytes 7012352 | tf_op jit(solution)/shard_map/dot_general | solution.py:11
  18.0 0.4 fusion.12
  18.5 1.1 fusion.13
  19.5 0.8 copy-done.6
  20.4 0.0 reduce-scatter.4.cloned.1.call-start
  20.4 0.5 reduce-scatter.4.cloned.1.call-update
  20.9 0.0 reduce-scatter.6.cloned.1.call-start
  21.0 0.5 reduce-scatter.6.cloned.1.call-update
  21.5 0.0 reduce-scatter.8.cloned.1.call-start
  21.6 0.5 reduce-scatter.8.cloned.1.call-update
  22.1 0.0 all-gather.12.cloned.1.call-start
  22.1 0.2 copy.33
  22.4 1.2 copy.32
  23.6 191.8 %all-reduce.3.cloned.1.call-done = (f32[64,2048]{1,0:T(8,128)}, f32[64,2048]{1,0:T(8,128)}) async-done(((f32[64,2048]{1,0:T(8,128)}, f32[64,2048]{1,0:T(8,128)}), (f32[64,2048]{1,0:T(8,128)}, f32[64,2048]{1,0:T(8,128)})) %all-reduce.3.cloned.1.call-update) | async-done | bytes 1048592 | tf_op jit(solution)/shard_map/psum | solution.py:68
  215.4 2.6 fusion.21
  218.0 0.0 all-gather.14.cloned.1.call-start
  218.1 1.6 copy.35
  219.7 1.6 copy.34
  221.3 4.5 fusion.19
  225.8 0.0 all-gather.6.cloned.1.call-start
  225.9 0.0 reduce-scatter.4.cloned.1.call-done
  225.9 3.9 fusion.24
  229.9 0.0 all-gather.8.cloned.1.call-start
  229.9 0.0 reduce-scatter.6.cloned.1.call-done
  230.0 4.9 %fusion.23 = (bf16[256,1536]{1,0:T(8,128)(2,1)}, f32[256,1536]{1,0:T(8,128)}, f32[256,1536]{1,0:T(8,128)}) fusion(f32[256,1536]{1,0:T(8,128)} %param.23, f32[256,1536]{1,0:T(8,128)} %reduce-scatter.6.cloned.1.call-done, f32[256,1536]{1,0:T(8,128)} %param.28), kind=kLoop, calls=%fused_computation.35 | loop fusion | flops 3538944 | bytes 8650752 | tf_op jit(solution)/shard_map/convert_element_type | solution.py:29
  234.9 0.0 all-gather.8.cloned.1.call-update
  234.9 0.0 all-gather.10.cloned.1.call-start
  235.0 0.0 reduce-scatter.8.cloned.1.call-done
  235.0 4.9 %fusion.22 = (bf16[256,1536]{1,0:T(8,128)(2,1)}, f32[256,1536]{1,0:T(8,128)}, f32[256,1536]{1,0:T(8,128)}) fusion(f32[256,1536]{1,0:T(8,128)} %param.24, f32[256,1536]{1,0:T(8,128)} %reduce-scatter.8.cloned.1.call-done, f32[256,1536]{1,0:T(8,128)} %param.29), kind=kLoop, calls=%fused_computation.34 | loop fusion | flops 3538944 | bytes 8650752 | tf_op jit(solution)/shard_map/convert_element_type | solution.py:29
  240.0 1.6 copy.39
  241.6 1.6 copy.41
  243.2 1.0 copy.38
  244.2 1.0 copy.40
  245.2 12.2 %all-gather.12.cloned.1.call-done = bf16[256,2048]{0,1:T(8,128)(2,1)} async-done(((bf16[256,512]{0,1:T(8,128)(2,1)}), bf16[256,2048]{0,1:T(8,128)(2,1)}) %all-gather.12.cloned.1.call-update) | async-done | bytes 1048592 | tf_op jit(solution)/shard_map/all_gather | solution.py:82
  257.4 2.3 copy.36
  259.7 44.0 %all-gather.14.cloned.1.call-done = bf16[768,2048]{0,1:T(8,128)(2,1)} async-done(((bf16[768,512]{0,1:T(8,128)(2,1)}), bf16[768,2048]{0,1:T(8,128)(2,1)}) %all-gather.14.cloned.1.call-update) | async-done | bytes 3145744 | tf_op jit(solution)/shard_map/all_gather | solution.py:83
  303.7 4.6 %copy.37 = bf16[768,2048]{1,0:T(8,128)(2,1)} copy(bf16[768,2048]{0,1:T(8,128)(2,1)} %all-gather.14.cloned.1.call-done) | data formatting | bytes 6291456
  308.3 33.0 %all-gather.6.cloned.1.call-done = bf16[256,4096]{1,0:T(8,128)(2,1)} async-done(((bf16[256,1024]{1,0:T(8,128)(2,1)}), bf16[256,4096]{1,0:T(8,128)(2,1)}) %all-gather.6.cloned.1.call-update) | async-done | bytes 2097168 | tf_op jit(solution)/shard_map/all_gather | solution.py:79
  341.3 46.1 %all-gather.8.cloned.1.call-done = bf16[256,6144]{1,0:T(8,128)(2,1)} async-done(((bf16[256,1536]{1,0:T(8,128)(2,1)}), bf16[256,6144]{1,0:T(8,128)(2,1)}) %all-gather.8.cloned.1.call-update) | async-done | bytes 3145744 | tf_op jit(solution)/shard_map/all_gather | solution.py:80
  387.4 46.1 %all-gather.10.cloned.1.call-done = bf16[256,6144]{1,0:T(8,128)(2,1)} async-done(((bf16[256,1536]{1,0:T(8,128)(2,1)}), bf16[256,6144]{1,0:T(8,128)(2,1)}) %all-gather.10.cloned.1.call-update) | async-done | bytes 3145744 | tf_op jit(solution)/shard_map/all_gather | solution.py:81
  433.5 3.3 copy.49
  436.8 1.7 copy.50
  438.5 1.4 copy-done.4
  439.8 1.7 copy.51
  441.5 1.1 copy-done.1
  (27 shorter events, 0.1 us)
Async XLA Ops:
  8.0 1.6 copy-start
  8.0 3.8 copy-start.10
  8.0 207.3 %all-reduce.3.cloned.1.call-start = ((), (), s32[]{:S(2)}) async-start(), calls=%async_computation.11 | async-start | bytes 2097152 | tf_op jit(solution)/shard_map/psum | solution.py:68
  11.8 6.2 %copy-start.7 = (f32[256,512]{1,0:T(8,128)S(1)}, f32[256,512]{1,0:T(8,128)}, u32[]{:S(2)}) copy-start(f32[256,512]{1,0:T(8,128)} %param.25) | copy-start | bytes 1572868
  11.8 6.1 %copy-start.12 = (f32[256,64]{0,1:T(8,128)S(1)}, f32[256,64]{0,1:T(8,128)}, u32[]{:S(2)}) copy-start(f32[256,64]{0,1:T(8,128)} %param.32) | copy-start | bytes 196612
  11.9 6.6 %copy-start.2 = (f32[768,512]{1,0:T(8,128)S(1)}, f32[768,512]{1,0:T(8,128)}, u32[]{:S(2)}) copy-start(f32[768,512]{1,0:T(8,128)} %param.26) | copy-start | bytes 4718596
  18.5 1.1 copy-start.5
  19.5 0.8 copy-start.6
  20.4 205.6 %reduce-scatter.4.cloned.1.call-start = ((), (), s32[]{:S(2)}) async-start(), calls=%async_computation.3 | async-start | bytes 5242880 | tf_op jit(solution)/shard_map/reduce_scatter | solution.py:55
  20.9 209.0 %reduce-scatter.6.cloned.1.call-start = ((), (), s32[]{:S(2)}) async-start(), calls=%async_computation.5 | async-start | bytes 7864320 | tf_op jit(solution)/shard_map/reduce_scatter | solution.py:56
  21.5 213.5 %reduce-scatter.8.cloned.1.call-start = ((), (), s32[]{:S(2)}) async-start(), calls=%async_computation.7 | async-start | bytes 7864320 | tf_op jit(solution)/shard_map/reduce_scatter | solution.py:57
  22.1 235.3 %all-gather.12.cloned.1.call-start = ((), (), s32[]{:S(2)}) async-start(), calls=%async_computation.9 | async-start | bytes 1310720 | tf_op jit(solution)/shard_map/all_gather | solution.py:82
  218.0 1.7 copy-start.11
  218.0 85.7 %all-gather.14.cloned.1.call-start = ((), (), s32[]{:S(2)}) async-start(), calls=%async_computation.10 | async-start | bytes 3932160 | tf_op jit(solution)/shard_map/all_gather | solution.py:83
  225.8 115.5 %all-gather.6.cloned.1.call-start = ((), (), s32[]{:S(2)}) async-start(), calls=%async_computation.4 | async-start | bytes 2621440 | tf_op jit(solution)/shard_map/all_gather | solution.py:79
  229.9 157.5 %all-gather.8.cloned.1.call-start = ((), (), s32[]{:S(2)}) async-start(), calls=%async_computation.6 | async-start | bytes 3932160 | tf_op jit(solution)/shard_map/all_gather | solution.py:80
  234.9 198.6 %all-gather.10.cloned.1.call-start = ((), (), s32[]{:S(2)}) async-start(), calls=%async_computation.8 | async-start | bytes 3932160 | tf_op jit(solution)/shard_map/all_gather | solution.py:81
  241.6 1.6 copy-start.9
  241.6 2.6 copy-start.8
  433.5 3.3 copy-start.3
  436.8 3.0 copy-start.4
  439.8 2.7 copy-start.1
Sparse Core Ops, SparseCore 0:
  20.5 194.8 all-reduce.2
Sparse Core Ops, SparseCore 1:
  23.8 56.6 reduce-scatter.3
  83.6 70.6 reduce-scatter.5
  157.3 71.7 reduce-scatter.7
  230.9 26.4 all-gather.11
  259.9 43.8 all-gather.13
  306.1 35.1 all-gather.5
  343.6 43.8 all-gather.7
  389.7 43.8 all-gather.9
where the time goes:
time: 450 us
  waiting for transfers between devices  375 us (83%)
  local copies, waits for them, and re-layouts  28.2 us (6%)
  matrix products  16.9 us (4%)
  between operations  15.8 us (4%)
  other arithmetic  13.8 us (3%)
    psum x1, waiting for transfers between devices, on_device(): totals = lax.psum((terms[0], terms[1]), ('rep', 'shard'))  192 us
    all_gather x1, waiting for transfers between devices, on_device(): lax.all_gather(a3, 'rep', axis=1, tiled=True)  46.1 us
    all_gather x1, waiting for transfers between devices, on_device(): lax.all_gather(a1, 'rep', axis=1, tiled=True)  46.1 us
    all_gather x1, waiting for transfers between devices, on_device(): lax.all_gather(a2, 'rep', axis=1, tiled=True)  44 us
    all_gather x1, waiting for transfers between devices, on_device(): lax.all_gather(a0, 'rep', axis=1, tiled=True)  33 us
    unnamed x39, local copies, waits for them, and re-layouts  28.2 us
    convert_element_type x3, other arithmetic, nesterov(): return (master.astype(jnp.bfloat16), master, moment_new)  13.8 us
    all_gather x1, waiting for transfers between devices, on_device(): lax.all_gather(ao, 'rep', axis=1, tiled=True)  12.2 us
  transfers between devices with their start and end apart: 9, of which 6 were waited for; matrix products, arithmetic and copies ran while one was open for 8% of the time, Pallas kernels for 0%

commit v1 on v0

v1 whole, which is shorter than its diff:
```python
import math

import jax
import jax.numpy as jnp
from jax import lax
from jax.experimental import pallas as pl
from jax.experimental.pallas import tpu as pltpu
from jax.sharding import PartitionSpec as P

rate_outer = 0.7
decay_moment = 0.9
inner_limit = 8.5
octaves = 124.0


def project(basis, matrix):
    return lax.dot_general(
        basis,
        matrix,
        (((0,), (0,)), ((), ())),
        precision=lax.Precision.HIGHEST,
        preferred_element_type=jnp.float32,
    )


def rebuild(basis, coeff):
    return jnp.dot(
        basis, coeff, precision=lax.Precision.HIGHEST, preferred_element_type=jnp.float32
    )


def nesterov(outer, moment, delta):
    moment_new = decay_moment * moment + delta
    master = outer - rate_outer * (delta + decay_moment * moment_new)
    return (master.astype(jnp.bfloat16), master, moment_new)


def pack(value, limit):
    slope = 2.0 * octaves * math.log(2.0) / limit
    size = jnp.exp(jnp.abs(value) * slope - octaves * math.log(2.0))
    return jnp.where(value < 0, -size, size).astype(jnp.bfloat16)


def unpack(code, limit):
    slope = limit / (2.0 * octaves * math.log(2.0))
    wide = code.astype(jnp.float32)
    size = (jnp.log(jnp.abs(wide)) + octaves * math.log(2.0)) * slope
    return jnp.where(wide < 0, -size, size)


def keep_wide(value, limit):
    return value


def swap(value, bit, axis):
    return lax.ppermute(value, axis, [(i, i ^ bit) for i in range(lax.axis_size(axis))])


def scatter_pairs(matrix, low, rows, first, second, encode, decode):
    me = lax.axis_index("rep")
    width = matrix.shape[1] // 4

    def block(owner):
        return lax.dynamic_slice(matrix, (low, owner * width), (rows, width))

    far = swap(encode(block(me ^ 3), inner_limit), first, "rep")
    near = swap(encode(block(me ^ first), inner_limit), first, "rep")
    relay = block(me ^ second) + decode(far, inner_limit)
    across = swap(encode(relay, 2 * inner_limit), second, "rep")
    return block(me) + decode(near, inner_limit) + decode(across, 2 * inner_limit)


def sum_columns(matrix):
    if lax.axis_size("rep") != 4:
        return lax.psum_scatter(matrix, "rep", scatter_dimension=1, tiled=True)
    half = matrix.shape[0] // 2
    return jnp.concatenate(
        [
            scatter_pairs(matrix, 0, half, 1, 2, pack, unpack),
            scatter_pairs(matrix, half, half, 2, 1, pack, unpack),
        ],
        axis=0,
    )


def place_kernel(own, by_x, by_y, far_top, far_low, out, sems):
    me = lax.axis_index("rep")
    rows, width = own.shape
    half = rows // 2

    def columns(owner):
        return pl.ds(pl.multiple_of(owner * width, 128), width)

    copies = [
        pltpu.make_async_copy(own, out.at[:, columns(me)], sems.at[0]),
        pltpu.make_async_copy(by_x, out.at[:, columns(me ^ 1)], sems.at[1]),
        pltpu.make_async_copy(by_y, out.at[:, columns(me ^ 2)], sems.at[2]),
        pltpu.make_async_copy(far_top, out.at[pl.ds(0, half), columns(me ^ 3)], sems.at[3]),
        pltpu.make_async_copy(far_low, out.at[pl.ds(half, half), columns(me ^ 3)], sems.at[4]),
    ]
    for copy in copies:
        copy.start()
    for copy in copies:
        copy.wait()


def gather_columns(own):
    if lax.axis_size("rep") != 4:
        return lax.all_gather(own, "rep", axis=1, tiled=True)
    rows, width = own.shape
    half = rows // 2
    by_x = swap(own, 1, "rep")
    by_y = swap(own, 2, "rep")
    far_top = swap(by_x[:half], 2, "rep")
    far_low = swap(by_y[half:], 1, "rep")
    return pl.pallas_call(
        place_kernel,
        out_shape=jax.ShapeDtypeStruct((rows, 4 * width), own.dtype),
        in_specs=[pl.BlockSpec(memory_space=pl.ANY)] * 5,
        out_specs=pl.BlockSpec(memory_space=pl.ANY),
        scratch_shapes=[pltpu.SemaphoreType.DMA((5,))],
        cost_estimate=pl.CostEstimate(
            flops=0, bytes_accessed=16 * rows * width, transcendentals=0
        ),
    )(own, by_x, by_y, far_top, far_low)


def coefficients(inner_out, inner_down, outer_out, outer_down, basis_out, basis_down):
    groups = lax.axis_size("rep")
    parts = (project(basis_out, inner_out), project(basis_down, inner_down))
    if groups == 4:
        rank = parts[0].shape[0]
        out_sum = scatter_pairs(parts[0], 0, rank, 1, 2, keep_wide, keep_wide)
        down_sum = scatter_pairs(parts[1], 0, rank, 2, 1, keep_wide, keep_wide)
    else:
        out_sum, down_sum = [
            lax.psum_scatter(part, "rep", scatter_dimension=1, tiled=True) for part in parts
        ]
    out_term = project(basis_out, outer_out) - out_sum / groups
    down_term = project(basis_down, outer_down) - down_sum / groups
    shards = lax.axis_size("shard")
    if shards & (shards - 1) or shards < 2:
        return lax.psum((out_term, down_term), "shard")
    even = lax.axis_index("shard") % 2 == 0
    total = jnp.where(even, out_term, down_term)
    total = total + swap(jnp.where(even, down_term, out_term), 1, "shard")
    bit = 2
    while bit < shards:
        total = total + swap(total, bit, "shard")
        bit *= 2
    other = swap(total, 1, "shard")
    return jnp.where(even, total, other), jnp.where(even, other, total)


def on_device(
    inner_wqkv,
    inner_w1,
    inner_w3,
    inner_wo,
    inner_w2,
    outer_wqkv,
    outer_w1,
    outer_w3,
    outer_wo,
    outer_w2,
    moment_wqkv,
    moment_w1,
    moment_w3,
    moment_wo,
    moment_w2,
    basis_wo,
    basis_w2,
):
    groups = lax.axis_size("rep")
    d_qkv = outer_wqkv - sum_columns(inner_wqkv[0]) / groups
    coeff_out, coeff_down = coefficients(
        inner_wo[0], inner_w2[0], outer_wo, outer_w2, basis_wo, basis_w2
    )
    d_one = outer_w1 - sum_columns(inner_w1[0]) / groups
    d_three = outer_w3 - sum_columns(inner_w3[0]) / groups
    d_out = rebuild(basis_wo, coeff_out)
    d_down = rebuild(basis_w2, coeff_down)
    a0, b0, c0 = nesterov(outer_wqkv, moment_wqkv, d_qkv)
    a1, b1, c1 = nesterov(outer_w1, moment_w1, d_one)
    a3, b3, c3 = nesterov(outer_w3, moment_w3, d_three)
    ao, bo, co = nesterov(outer_wo, moment_wo, d_out)
    a2, b2, c2 = nesterov(outer_w2, moment_w2, d_down)
    return (
        gather_columns(a0),
        gather_columns(a1),
        gather_columns(a3),
        gather_columns(ao),
        gather_columns(a2),
        b0,
        b1,
        b3,
        bo,
        b2,
        c0,
        c1,
        c3,
        co,
        c2,
    )


def solution(mesh):
    inner = P("rep", "shard", None)
    owned = P("shard", "rep")
    shared = P("shard", None)
    return jax.shard_map(
        on_device,
        mesh=mesh,
        in_specs=(inner,) * 5 + (owned,) * 10 + (shared,) * 2,
        out_specs=(shared,) * 5 + (owned,) * 10,
        check_vma=False,
    )
```

time: 450 us -> 620 us (1.38)
  Pallas kernels: 0 us -> 387 us
  waiting for transfers between devices: 375 us -> 121 us
  starting transfers between devices: 0.38 us -> 56.8 us
  local copies, waits for them, and re-layouts: 28.2 us -> 10.2 us
  other arithmetic: 13.8 us -> 28.6 us
  between operations: 15.8 us -> 1.33 us
    pallas_call x0 -> x5, Pallas kernels: none -> 387 us  [gather_columns(): pl.pallas_call(place_kernel, out_shape=jax.ShapeDtypeStruct((rows, 4 * wi...]
    psum x1 -> x0, waiting for transfers between devices: 192 us -> none  [on_device(): totals = lax.psum((terms[0], terms[1]), ('rep', 'shard'))]
    all_gather x5 -> x0, waiting for transfers between devices: 181 us -> none  [the longest x1 46.1 us: on_device(): lax.all_gather(a3, 'rep', axis=1, tiled=True)]
    ppermute x0 -> x48, waiting for transfers between devices: none -> 121 us  [swap(): lax.ppermute(value, axis, [(i, i ^ bit) for i in range(lax.axis_size(axis...]
    ppermute x0 -> x48, starting transfers between devices: none -> 56.8 us  [swap(): lax.ppermute(value, axis, [(i, i ^ bit) for i in range(lax.axis_size(axis...]
    unnamed x39 -> x86, local copies, waits for them, and re-layouts: 28.2 us -> 5.44 us
    convert_element_type x0 -> x9, other arithmetic: none -> 13.6 us  [pack(): return jnp.where(value < 0, -size, size).astype(jnp.bfloat16)]
    convert_element_type x3, other arithmetic: 13.8 us -> 6.42 us  [nesterov(): return (master.astype(jnp.bfloat16), master, moment_new)]
  transfers between devices with their start and end apart: 9 -> 48, of which waited for: 6 -> 17; matrix products, arithmetic and copies ran while one was open for 8% -> 7% of each run, Pallas kernels for 0% -> 47%
where the time goes in v1:
time: 620 us
  Pallas kernels  387 us (62%)
  waiting for transfers between devices  121 us (20%)
  starting transfers between devices  56.8 us (9%)
  other arithmetic  28.6 us (5%)
  matrix products  15.7 us (3%)
  local copies, waits for them, and re-layouts  10.2 us (2%)
    pallas_call x5, Pallas kernels, gather_columns(): pl.pallas_call(place_kernel, out_shape=jax.ShapeDtypeStruct((rows, 4 * wi...  387 us
    ppermute x48, waiting for transfers between devices, swap(): lax.ppermute(value, axis, [(i, i ^ bit) for i in range(lax.axis_size(axis...  121 us
    ppermute x48, starting transfers between devices, swap(): lax.ppermute(value, axis, [(i, i ^ bit) for i in range(lax.axis_size(axis...  56.8 us
    convert_element_type x9, other arithmetic, pack(): return jnp.where(value < 0, -size, size).astype(jnp.bfloat16)  13.6 us
  transfers between devices with their start and end apart: 48, of which 17 were waited for; matrix products, arithmetic and copies ran while one was open for 7% of the time, Pallas kernels for 47%

profile of v1, /device:TPU:0, one launch (start us, length us, event | category | flops | bytes accessed | tf_op | source)
XLA Modules:
  0.0 620.1 jit_solution(11050778652193818154)
XLA Ops:
  0.7 1.6 copy-done
  2.2 2.3 fusion.2
  5.2 2.9 collective-permute-start.31
  8.2 6.2 fusion
  15.1 1.5 collective-permute-start.34
  17.2 1.9 fusion.90
  19.1 2.0 collective-permute-start.1
  21.5 1.7 fusion.111
  23.2 2.1 fusion.60
  25.3 1.6 dynamic-slice_add_fusion.1
  26.9 1.5 collective-permute-start.32
  28.4 1.6 dynamic-slice_add_fusion
  30.5 2.1 fusion.48
  34.7 1.9 collective-permute-done.35
  38.0 1.9 fusion.92
  40.6 1.7 collective-permute-start.37
  42.3 2.6 collective-permute-done.21
  44.9 2.1 fusion.62
  47.0 1.5 collective-permute-start.20
  49.1 9.9 %collective-permute-done = bf16[128,1024]{1,0:T(8,128)(2,1)S(1)} collective-permute-done((bf16[128,1024]{1,0:T(8,128)(2,1)S(1)}, bf16[128,1024]{1,0:T(8,128)(2,1)S(1)}, u32[]{:S(2)}, u32[]{:S(2)}) %collective-permute-start) | collective-permute-done | bytes 262176 | tf_op jit(solution)/shard_map/ppermute | solution.py:56
  59.0 2.6 collective-permute-start.38
  62.8 2.2 fusion.50
  65.0 1.5 collective-permute-start.10
  68.1 3.2 collective-permute-done.4
  73.3 3.4 fusion.104
  82.8 1.7 fusion.106
  87.9 1.9 fusion.109
  89.8 19.0 %collective-permute-done.24 = bf16[128,1536]{1,0:T(8,128)(2,1)S(1)} collective-permute-done((bf16[128,1536]{1,0:T(8,128)(2,1)S(1)}, bf16[128,1536]{1,0:T(8,128)(2,1)S(1)}, u32[]{:S(2)}, u32[]{:S(2)}) %collective-permute-start.24) | collective-permute-done | bytes 393248 | tf_op jit(solution)/shard_map/ppermute | solution.py:56
  110.5 15.0 %collective-permute-done.14 = bf16[128,1536]{1,0:T(8,128)(2,1)S(1)} collective-permute-done((bf16[128,1536]{1,0:T(8,128)(2,1)S(1)}, bf16[128,1536]{1,0:T(8,128)(2,1)S(1)}, u32[]{:S(2)}, u32[]{:S(2)}) %collective-permute-start.14) | collective-permute-done | bytes 393248 | tf_op jit(solution)/shard_map/ppermute | solution.py:56
  128.2 9.5 %collective-permute-done.25 = bf16[128,1536]{1,0:T(8,128)(2,1)S(1)} collective-permute-done((bf16[128,1536]{1,0:T(8,128)(2,1)S(1)}, bf16[128,1536]{1,0:T(8,128)(2,1)S(1)}, u32[]{:S(2)}, u32[]{:S(2)}) %collective-permute-start.25) | collective-permute-done | bytes 393248 | tf_op jit(solution)/shard_map/ppermute | solution.py:56
  139.6 2.3 fusion.107
  142.5 13.2 %collective-permute-done.15 = bf16[128,1536]{1,0:T(8,128)(2,1)S(1)} collective-permute-done((bf16[128,1536]{1,0:T(8,128)(2,1)S(1)}, bf16[128,1536]{1,0:T(8,128)(2,1)S(1)}, u32[]{:S(2)}, u32[]{:S(2)}) %collective-permute-start.15) | collective-permute-done | bytes 393248 | tf_op jit(solution)/shard_map/ppermute | solution.py:56
  159.0 2.1 collective-permute-start.7
  161.1 3.8 collective-permute-done.41.by_y
  167.5 2.3 fusion.108
  169.8 6.4 %collective-permute-done.7.by_y = bf16[256,1024]{1,0:T(8,128)(2,1)S(1)} collective-permute-done((bf16[256,1024]{1,0:T(8,128)(2,1)S(1)}, bf16[256,1024]{1,0:T(8,128)(2,1)S(1)}, u32[]{:S(2)}, u32[]{:S(2)}) %collective-permute-start.7) | collective-permute-done | bytes 524320 | tf_op jit(solution)/shard_map/ppermute | solution.py:56
  179.9 5.2 collective-permute-done.26.by_x
  186.5 6.5 %collective-permute-done.27.by_y = bf16[256,1536]{1,0:T(8,128)(2,1)S(1)} collective-permute-done((bf16[256,1536]{1,0:T(8,128)(2,1)S(1)}, bf16[256,1536]{1,0:T(8,128)(2,1)S(1)}, u32[]{:S(2)}, u32[]{:S(2)}) %collective-permute-start.27) | collective-permute-done | bytes 786464 | tf_op jit(solution)/shard_map/ppermute | solution.py:56
  194.6 1.8 collective-permute-done.16.by_x
  197.8 12.1 %collective-permute-done.17.by_y = bf16[256,1536]{1,0:T(8,128)(2,1)S(1)} collective-permute-done((bf16[256,1536]{1,0:T(8,128)(2,1)S(1)}, bf16[256,1536]{1,0:T(8,128)(2,1)S(1)}, u32[]{:S(2)}, u32[]{:S(2)}) %collective-permute-start.17) | collective-permute-done | bytes 786464 | tf_op jit(solution)/shard_map/ppermute | solution.py:56
  214.6 7.9 %collective-permute-done.42.far_top = bf16[128,512]{1,0:T(8,128)(2,1)S(1)} collective-permute-done((bf16[128,512]{1,0:T(8,128)(2,1)S(1)}, bf16[128,512]{1,0:T(8,128)(2,1)S(1)}, u32[]{:S(2)}, u32[]{:S(2)}) %collective-permute-start.42) | collective-permute-done | bytes 131104 | tf_op jit(solution)/shard_map/ppermute | solution.py:56
  222.5 2.5 collective-permute-start.47
  227.2 2.0 collective-permute-start.19
  229.2 32.9 %shard_map.283 = bf16[256,2048]{1,0:T(8,128)(2,1)} custom-call(bf16[256,512]{1,0:T(8,128)(2,1)} %copy-done.25, bf16[256,512]{1,0:T(8,128)(2,1)} %copy-done.26, bf16[256,512]{1,0:T(8,128)(2,1)} %copy-done.27, bf16[128,512]{1,0:T(8,128)(2,1)} %copy-done.38, bf16[128,512]{1,0:T(8,128)(2,1)} %collective-permute-done.43.far_low), custom_call_target="tpu_custom_call" | custom-call | bytes 2097152 | tf_op jit(solution)/shard_map/pallas_call | solution.py:116
  262.1 64.7 %shard_map.280 = bf16[256,4096]{1,0:T(8,128)(2,1)} custom-call(bf16[256,1024]{1,0:T(8,128)(2,1)} %copy-done.8, bf16[256,1024]{1,0:T(8,128)(2,1)} %copy-done.21, bf16[256,1024]{1,0:T(8,128)(2,1)} %copy-done.22, bf16[128,1024]{1,0:T(8,128)(2,1)} %copy-done.36, bf16[128,1024]{1,0:T(8,128)(2,1)} %copy-done.37), custom_call_target="tpu_custom_call" | custom-call | bytes 4194304 | tf_op jit(solution)/shard_map/pallas_call | solution.py:116
  327.5 96.4 %shard_map.284 = bf16[768,2048]{1,0:T(8,128)(2,1)} custom-call(bf16[768,512]{1,0:T(8,128)(2,1)} %copy-done.6, bf16[768,512]{1,0:T(8,128)(2,1)} %copy-done.9, bf16[768,512]{1,0:T(8,128)(2,1)} %copy-done.10, bf16[384,512]{1,0:T(8,128)(2,1)} %copy-done.30, bf16[384,512]{1,0:T(8,128)(2,1)} %copy-done.33), custom_call_target="tpu_custom_call" | custom-call | bytes 6291456 | tf_op jit(solution)/shard_map/pallas_call | solution.py:116
  425.5 96.4 %shard_map.282 = bf16[256,6144]{1,0:T(8,128)(2,1)} custom-call(bf16[256,1536]{1,0:T(8,128)(2,1)} %copy-done.4, bf16[256,1536]{1,0:T(8,128)(2,1)} %copy-done.11, bf16[256,1536]{1,0:T(8,128)(2,1)} %copy-done.12, bf16[128,1536]{1,0:T(8,128)(2,1)} %copy-done.31, bf16[128,1536]{1,0:T(8,128)(2,1)} %copy-done.34), custom_call_target="tpu_custom_call" | custom-call | bytes 6291456 | tf_op jit(solution)/shard_map/pallas_call | solution.py:116
  523.5 96.4 %shard_map.281 = bf16[256,6144]{1,0:T(8,128)(2,1)} custom-call(bf16[256,1536]{1,0:T(8,128)(2,1)} %copy-done.5, bf16[256,1536]{1,0:T(8,128)(2,1)} %copy-done.13, bf16[256,1536]{1,0:T(8,128)(2,1)} %copy-done.14, bf16[128,1536]{1,0:T(8,128)(2,1)} %copy-done.32, bf16[128,1536]{1,0:T(8,128)(2,1)} %copy-done.35), custom_call_target="tpu_custom_call" | custom-call | bytes 6291456 | tf_op jit(solution)/shard_map/pallas_call | solution.py:116
  (183 shorter events, 53.2 us)
Async XLA Ops:
  5.2 20.1 %collective-permute-start.31 = (f32[64,512]{1,0:T(8,128)}, f32[64,512]{1,0:T(8,128)}, u32[]{:S(2)}, u32[]{:S(2)}) collective-permute-start(f32[64,512]{1,0:T(8,128)} %get-tuple-element.51), channel_id=1, source_target_pairs={{0,8},{8,0},{16,24},{24,16},{1,9},{9,1},{17,25},{25,17},{2,10},{10... | collective-permute-start | bytes 393224 | tf_op jit(solution)/shard_map/ppermute | solution.py:56
  15.1 13.3 %collective-permute-start.34 = (f32[64,512]{1,0:T(8,128)}, f32[64,512]{1,0:T(8,128)}, u32[]{:S(2)}, u32[]{:S(2)}) collective-permute-start(f32[64,512]{1,0:T(8,128)} %get-tuple-element.49), channel_id=1, source_target_pairs={{0,16},{8,24},{16,0},{24,8},{1,17},{9,25},{17,1},{25,9},{2,18},{10... | collective-permute-start | bytes 393224 | tf_op jit(solution)/shard_map/ppermute | solution.py:56
  16.6 16.0 %collective-permute-start.30 = (f32[64,512]{1,0:T(8,128)}, f32[64,512]{1,0:T(8,128)}, u32[]{:S(2)}, u32[]{:S(2)}) collective-permute-start(f32[64,512]{1,0:T(8,128)} %get-tuple-element.50), channel_id=1, source_target_pairs={{0,8},{8,0},{16,24},{24,16},{1,9},{9,1},{17,25},{25,17},{2,10},{10... | collective-permute-start | bytes 393224 | tf_op jit(solution)/shard_map/ppermute | solution.py:56
  17.2 17.0 %collective-permute-start.33 = (f32[64,512]{1,0:T(8,128)}, f32[64,512]{1,0:T(8,128)}, u32[]{:S(2)}, u32[]{:S(2)}) collective-permute-start(f32[64,512]{1,0:T(8,128)} %get-tuple-element.48), channel_id=1, source_target_pairs={{0,16},{8,24},{16,0},{24,8},{1,17},{9,25},{17,1},{25,9},{2,18},{10... | collective-permute-start | bytes 393224 | tf_op jit(solution)/shard_map/ppermute | solution.py:56
  19.1 18.9 %collective-permute-start.1 = (bf16[128,1024]{1,0:T(8,128)(2,1)}, bf16[128,1024]{1,0:T(8,128)(2,1)}, u32[]{:S(2)}, u32[]{:S(2)}) collective-permute-start(bf16[128,1024]{1,0:T(8,128)(2,1)} %fusion.90), channel_id=1, source_target_pairs={{0,8},{8,0},{16,24},{24,16},{1,9},{9,1},{17,25},{25,17},{2,10},{10... | collective-permute-start | bytes 786440 | tf_op jit(solution)/shard_map/ppermute | solution.py:56
  26.9 7.8 %collective-permute-start.32 = (f32[64,512]{1,0:T(8,128)}, f32[64,512]{1,0:T(8,128)}, u32[]{:S(2)}, u32[]{:S(2)}) collective-permute-start(f32[64,512]{1,0:T(8,128)} %dynamic-slice_add_fusion.1), channel_id=1, source_target_pairs={{0,16},{8,24},{16,0},{24,8},{1,17},{9,25},{17,1},{25,9},{2,18},{10... | collective-permute-start | bytes 393224 | tf_op jit(solution)/shard_map/ppermute | solution.py:56
  30.0 6.6 %collective-permute-start.35 = (f32[64,512]{1,0:T(8,128)}, f32[64,512]{1,0:T(8,128)}, u32[]{:S(2)}, u32[]{:S(2)}) collective-permute-start(f32[64,512]{1,0:T(8,128)} %dynamic-slice_add_fusion), channel_id=1, source_target_pairs={{0,8},{8,0},{16,24},{24,16},{1,9},{9,1},{17,25},{25,17},{2,10},{10... | collective-permute-start | bytes 393224 | tf_op jit(solution)/shard_map/ppermute | solution.py:56
  32.6 12.3 %collective-permute-start.21 = (bf16[128,1536]{1,0:T(8,128)(2,1)}, bf16[128,1536]{1,0:T(8,128)(2,1)S(1)}, u32[]{:S(2)}, u32[]{:S(2)}) collective-permute-start(bf16[128,1536]{1,0:T(8,128)(2,1)} %fusion.60), channel_id=1, source_target_pairs={{0,8},{8,0},{16,24},{24,16},{1,9},{9,1},{17,25},{25,17},{2,10},{10... | collective-permute-start | bytes 1179656 | tf_op jit(solution)/shard_map/ppermute | solution.py:56
  34.1 28.7 %collective-permute-start.11 = (bf16[128,1536]{1,0:T(8,128)(2,1)}, bf16[128,1536]{1,0:T(8,128)(2,1)S(1)}, u32[]{:S(2)}, u32[]{:S(2)}) collective-permute-start(bf16[128,1536]{1,0:T(8,128)(2,1)} %fusion.48), channel_id=1, source_target_pairs={{0,8},{8,0},{16,24},{24,16},{1,9},{9,1},{17,25},{25,17},{2,10},{10... | collective-permute-start | bytes 1179656 | tf_op jit(solution)/shard_map/ppermute | solution.py:56
  37.9 2.7 collective-permute-start.36
  39.9 19.1 %collective-permute-start = (bf16[128,1024]{1,0:T(8,128)(2,1)S(1)}, bf16[128,1024]{1,0:T(8,128)(2,1)S(1)}, u32[]{:S(2)}, u32[]{:S(2)}) collective-permute-start(bf16[128,1024]{1,0:T(8,128)(2,1)S(1)} %get-tuple-element.47), channel_id=1, source_target_pairs={{0,8},{8,0},{16,24},{24,16},{1,9},{9,1},{17,25},{25,17},{2,10},{10... | collective-permute-start | bytes 786440 | tf_op jit(solution)/shard_map/ppermute | solution.py:56
  40.1 21.4 %collective-permute-start.2 = (bf16[128,1024]{1,0:T(8,128)(2,1)S(1)}, bf16[128,1024]{1,0:T(8,128)(2,1)S(1)}, u32[]{:S(2)}, u32[]{:S(2)}) collective-permute-start(bf16[128,1024]{1,0:T(8,128)(2,1)S(1)} %get-tuple-element.46), channel_id=1, source_target_pairs={{0,16},{8,24},{16,0},{24,8},{1,17},{9,25},{17,1},{25,9},{2,18},{10... | collective-permute-start | bytes 786440 | tf_op jit(solution)/shard_map/ppermute | solution.py:56
  40.6 7.9 %collective-permute-start.37 = (f32[64,512]{1,0:T(8,128)S(1)}, f32[64,512]{1,0:T(8,128)S(1)}, u32[]{:S(2)}, u32[]{:S(2)}) collective-permute-start(f32[64,512]{1,0:T(8,128)S(1)} %select_add_fusion), channel_id=1, source_target_pairs={{0,2},{1,3},{2,0},{3,1},{4,6},{5,7},{6,4},{7,5},{8,10},{9,11},{10,... | collective-permute-start | bytes 393224 | tf_op jit(solution)/shard_map/ppermute | solution.py:56
  47.0 29.7 %collective-permute-start.20 = (bf16[128,1536]{1,0:T(8,128)(2,1)S(1)}, bf16[128,1536]{1,0:T(8,128)(2,1)S(1)}, u32[]{:S(2)}, u32[]{:S(2)}) collective-permute-start(bf16[128,1536]{1,0:T(8,128)(2,1)S(1)} %get-tuple-element.37), channel_id=1, source_target_pairs={{0,8},{8,0},{16,24},{24,16},{1,9},{9,1},{17,25},{25,17},{2,10},{10... | collective-permute-start | bytes 1179656 | tf_op jit(solution)/shard_map/ppermute | solution.py:56
  48.5 29.6 %collective-permute-start.22 = (bf16[128,1536]{1,0:T(8,128)(2,1)S(1)}, bf16[128,1536]{1,0:T(8,128)(2,1)S(1)}, u32[]{:S(2)}, u32[]{:S(2)}) collective-permute-start(bf16[128,1536]{1,0:T(8,128)(2,1)S(1)} %get-tuple-element.36), channel_id=1, source_target_pairs={{0,16},{8,24},{16,0},{24,8},{1,17},{9,25},{17,1},{25,9},{2,18},{10... | collective-permute-start | bytes 1179656 | tf_op jit(solution)/shard_map/ppermute | solution.py:56
  59.0 7.6 %collective-permute-start.38 = (f32[64,512]{1,0:T(8,128)S(1)}, f32[64,512]{1,0:T(8,128)S(1)}, u32[]{:S(2)}, u32[]{:S(2)}) collective-permute-start(f32[64,512]{1,0:T(8,128)S(1)} %add.317), channel_id=1, source_target_pairs={{0,4},{1,5},{2,6},{3,7},{4,0},{5,1},{6,2},{7,3},{8,12},{9,13},{10,... | collective-permute-start | bytes 393224 | tf_op jit(solution)/shard_map/ppermute | solution.py:56
  62.2 9.1 %collective-permute-start.4 = (bf16[128,1024]{1,0:T(8,128)(2,1)S(1)}, bf16[128,1024]{1,0:T(8,128)(2,1)S(1)}, u32[]{:S(2)}, u32[]{:S(2)}) collective-permute-start(bf16[128,1024]{1,0:T(8,128)(2,1)S(1)} %get-tuple-element.45), channel_id=1, source_target_pairs={{0,16},{8,24},{16,0},{24,8},{1,17},{9,25},{17,1},{25,9},{2,18},{10... | collective-permute-start | bytes 786440 | tf_op jit(solution)/shard_map/ppermute | solution.py:56
  65.0 14.7 %collective-permute-start.10 = (bf16[128,1536]{1,0:T(8,128)(2,1)S(1)}, bf16[128,1536]{1,0:T(8,128)(2,1)S(1)}, u32[]{:S(2)}, u32[]{:S(2)}) collective-permute-start(bf16[128,1536]{1,0:T(8,128)(2,1)S(1)} %get-tuple-element.42), channel_id=1, source_target_pairs={{0,8},{8,0},{16,24},{24,16},{1,9},{9,1},{17,25},{25,17},{2,10},{10... | collective-permute-start | bytes 1179656 | tf_op jit(solution)/shard_map/ppermute | solution.py:56
  66.6 14.6 %collective-permute-start.12 = (bf16[128,1536]{1,0:T(8,128)(2,1)S(1)}, bf16[128,1536]{1,0:T(8,128)(2,1)S(1)}, u32[]{:S(2)}, u32[]{:S(2)}) collective-permute-start(bf16[128,1536]{1,0:T(8,128)(2,1)S(1)} %get-tuple-element.41), channel_id=1, source_target_pairs={{0,16},{8,24},{16,0},{24,8},{1,17},{9,25},{17,1},{25,9},{2,18},{10... | collective-permute-start | bytes 1179656 | tf_op jit(solution)/shard_map/ppermute | solution.py:56
  71.3 1.3 collective-permute-start.39
  72.6 11.9 %collective-permute-start.3 = (bf16[128,1024]{1,0:T(8,128)(2,1)S(1)}, bf16[128,1024]{1,0:T(8,128)(2,1)S(1)}, u32[]{:S(2)}, u32[]{:S(2)}) collective-permute-start(bf16[128,1024]{1,0:T(8,128)(2,1)S(1)} %get-tuple-element.44), channel_id=1, source_target_pairs={{0,16},{8,24},{16,0},{24,8},{1,17},{9,25},{17,1},{25,9},{2,18},{10... | collective-permute-start | bytes 786440 | tf_op jit(solution)/shard_map/ppermute | solution.py:56
  76.7 9.2 %collective-permute-start.5 = (bf16[128,1024]{1,0:T(8,128)(2,1)S(1)}, bf16[128,1024]{1,0:T(8,128)(2,1)S(1)}, u32[]{:S(2)}, u32[]{:S(2)}) collective-permute-start(bf16[128,1024]{1,0:T(8,128)(2,1)S(1)} %fusion.98), channel_id=1, source_target_pairs={{0,8},{8,0},{16,24},{24,16},{1,9},{9,1},{17,25},{25,17},{2,10},{10... | collective-permute-start | bytes 786440 | tf_op jit(solution)/shard_map/ppermute | solution.py:56
  78.2 99.5 %collective-permute-start.44 = (bf16[768,512]{1,0:T(8,128)(2,1)S(1)}, bf16[768,512]{1,0:T(8,128)(2,1)S(1)}, u32[]{:S(2)}, u32[]{:S(2)}) collective-permute-start(bf16[768,512]{1,0:T(8,128)(2,1)S(1)} %get-tuple-element.15.own), channel_id=1, source_target_pairs={{0,8},{8,0},{16,24},{24,16},{1,9},{9,1},{17,25},{25,17},{2,10},{10... | collective-permute-start | bytes 2359304 | tf_op jit(solution)/shard_map/ppermute | solution.py:56
  79.7 99.0 %collective-permute-start.45 = (bf16[768,512]{1,0:T(8,128)(2,1)S(1)}, bf16[768,512]{1,0:T(8,128)(2,1)S(1)}, u32[]{:S(2)}, u32[]{:S(2)}) collective-permute-start(bf16[768,512]{1,0:T(8,128)(2,1)S(1)} %get-tuple-element.15.own), channel_id=1, source_target_pairs={{0,16},{8,24},{16,0},{24,8},{1,17},{9,25},{17,1},{25,9},{2,18},{10... | collective-permute-start | bytes 2359304 | tf_op jit(solution)/shard_map/ppermute | solution.py:56
  81.1 27.6 %collective-permute-start.24 = (bf16[128,1536]{1,0:T(8,128)(2,1)S(1)}, bf16[128,1536]{1,0:T(8,128)(2,1)S(1)}, u32[]{:S(2)}, u32[]{:S(2)}) collective-permute-start(bf16[128,1536]{1,0:T(8,128)(2,1)S(1)} %get-tuple-element.35), channel_id=1, source_target_pairs={{0,16},{8,24},{16,0},{24,8},{1,17},{9,25},{17,1},{25,9},{2,18},{10... | collective-permute-start | bytes 1179656 | tf_op jit(solution)/shard_map/ppermute | solution.py:56
  84.5 43.0 %collective-permute-start.23 = (bf16[128,1536]{1,0:T(8,128)(2,1)S(1)}, bf16[128,1536]{1,0:T(8,128)(2,1)S(1)}, u32[]{:S(2)}, u32[]{:S(2)}) collective-permute-start(bf16[128,1536]{1,0:T(8,128)(2,1)S(1)} %get-tuple-element.34), channel_id=1, source_target_pairs={{0,16},{8,24},{16,0},{24,8},{1,17},{9,25},{17,1},{25,9},{2,18},{10... | collective-permute-start | bytes 1179656 | tf_op jit(solution)/shard_map/ppermute | solution.py:56
  85.9 39.7 %collective-permute-start.14 = (bf16[128,1536]{1,0:T(8,128)(2,1)S(1)}, bf16[128,1536]{1,0:T(8,128)(2,1)S(1)}, u32[]{:S(2)}, u32[]{:S(2)}) collective-permute-start(bf16[128,1536]{1,0:T(8,128)(2,1)S(1)} %get-tuple-element.40), channel_id=1, source_target_pairs={{0,16},{8,24},{16,0},{24,8},{1,17},{9,25},{17,1},{25,9},{2,18},{10... | collective-permute-start | bytes 1179656 | tf_op jit(solution)/shard_map/ppermute | solution.py:56
  108.7 33.2 %collective-permute-start.13 = (bf16[128,1536]{1,0:T(8,128)(2,1)S(1)}, bf16[128,1536]{1,0:T(8,128)(2,1)S(1)}, u32[]{:S(2)}, u32[]{:S(2)}) collective-permute-start(bf16[128,1536]{1,0:T(8,128)(2,1)S(1)} %get-tuple-element.39), channel_id=1, source_target_pairs={{0,16},{8,24},{16,0},{24,8},{1,17},{9,25},{17,1},{25,9},{2,18},{10... | collective-permute-start | bytes 1179656 | tf_op jit(solution)/shard_map/ppermute | solution.py:56
  125.6 12.1 %collective-permute-start.25 = (bf16[128,1536]{1,0:T(8,128)(2,1)S(1)}, bf16[128,1536]{1,0:T(8,128)(2,1)S(1)}, u32[]{:S(2)}, u32[]{:S(2)}) collective-permute-start(bf16[128,1536]{1,0:T(8,128)(2,1)S(1)} %fusion.68), channel_id=1, source_target_pairs={{0,8},{8,0},{16,24},{24,16},{1,9},{9,1},{17,25},{25,17},{2,10},{10... | collective-permute-start | bytes 1179656 | tf_op jit(solution)/shard_map/ppermute | solution.py:56
  127.5 38.9 %collective-permute-start.6 = (bf16[256,1024]{1,0:T(8,128)(2,1)S(1)}, bf16[256,1024]{1,0:T(8,128)(2,1)S(1)}, u32[]{:S(2)}, u32[]{:S(2)}) collective-permute-start(bf16[256,1024]{1,0:T(8,128)(2,1)S(1)} %get-tuple-element.30.own), channel_id=1, source_target_pairs={{0,8},{8,0},{16,24},{24,16},{1,9},{9,1},{17,25},{25,17},{2,10},{10... | collective-permute-start | bytes 1572872 | tf_op jit(solution)/shard_map/ppermute | solution.py:56
  137.6 18.1 %collective-permute-start.15 = (bf16[128,1536]{1,0:T(8,128)(2,1)S(1)}, bf16[128,1536]{1,0:T(8,128)(2,1)S(1)}, u32[]{:S(2)}, u32[]{:S(2)}) collective-permute-start(bf16[128,1536]{1,0:T(8,128)(2,1)S(1)} %fusion.56), channel_id=1, source_target_pairs={{0,8},{8,0},{16,24},{24,16},{1,9},{9,1},{17,25},{25,17},{2,10},{10... | collective-permute-start | bytes 1179656 | tf_op jit(solution)/shard_map/ppermute | solution.py:56
  141.9 17.1 %collective-permute-start.40 = (bf16[256,512]{1,0:T(8,128)(2,1)S(1)}, bf16[256,512]{1,0:T(8,128)(2,1)S(1)}, u32[]{:S(2)}, u32[]{:S(2)}) collective-permute-start(bf16[256,512]{1,0:T(8,128)(2,1)S(1)} %get-tuple-element.18.own), channel_id=1, source_target_pairs={{0,8},{8,0},{16,24},{24,16},{1,9},{9,1},{17,25},{25,17},{2,10},{10... | collective-permute-start | bytes 786440 | tf_op jit(solution)/shard_map/ppermute | solution.py:56
  155.7 9.2 %collective-permute-start.41 = (bf16[256,512]{1,0:T(8,128)(2,1)S(1)}, bf16[256,512]{1,0:T(8,128)(2,1)S(1)}, u32[]{:S(2)}, u32[]{:S(2)}) collective-permute-start(bf16[256,512]{1,0:T(8,128)(2,1)S(1)} %get-tuple-element.18.own), channel_id=1, source_target_pairs={{0,16},{8,24},{16,0},{24,8},{1,17},{9,25},{17,1},{25,9},{2,18},{10... | collective-permute-start | bytes 786440 | tf_op jit(solution)/shard_map/ppermute | solution.py:56
  159.0 17.2 %collective-permute-start.7 = (bf16[256,1024]{1,0:T(8,128)(2,1)S(1)}, bf16[256,1024]{1,0:T(8,128)(2,1)S(1)}, u32[]{:S(2)}, u32[]{:S(2)}) collective-permute-start(bf16[256,1024]{1,0:T(8,128)(2,1)S(1)} %get-tuple-element.30.own), channel_id=1, source_target_pairs={{0,16},{8,24},{16,0},{24,8},{1,17},{9,25},{17,1},{25,9},{2,18},{10... | collective-permute-start | bytes 1572872 | tf_op jit(solution)/shard_map/ppermute | solution.py:56
  164.9 20.1 %collective-permute-start.26 = (bf16[256,1536]{1,0:T(8,128)(2,1)S(1)}, bf16[256,1536]{1,0:T(8,128)(2,1)S(1)}, u32[]{:S(2)}, u32[]{:S(2)}) collective-permute-start(bf16[256,1536]{1,0:T(8,128)(2,1)S(1)} %get-tuple-element.24.own), channel_id=1, source_target_pairs={{0,8},{8,0},{16,24},{24,16},{1,9},{9,1},{17,25},{25,17},{2,10},{10... | collective-permute-start | bytes 2359304 | tf_op jit(solution)/shard_map/ppermute | solution.py:56
  166.4 26.6 %collective-permute-start.27 = (bf16[256,1536]{1,0:T(8,128)(2,1)S(1)}, bf16[256,1536]{1,0:T(8,128)(2,1)S(1)}, u32[]{:S(2)}, u32[]{:S(2)}) collective-permute-start(bf16[256,1536]{1,0:T(8,128)(2,1)S(1)} %get-tuple-element.24.own), channel_id=1, source_target_pairs={{0,16},{8,24},{16,0},{24,8},{1,17},{9,25},{17,1},{25,9},{2,18},{10... | collective-permute-start | bytes 2359304 | tf_op jit(solution)/shard_map/ppermute | solution.py:56
  176.2 20.1 %collective-permute-start.16 = (bf16[256,1536]{1,0:T(8,128)(2,1)S(1)}, bf16[256,1536]{1,0:T(8,128)(2,1)S(1)}, u32[]{:S(2)}, u32[]{:S(2)}) collective-permute-start(bf16[256,1536]{1,0:T(8,128)(2,1)S(1)} %get-tuple-element.27.own), channel_id=1, source_target_pairs={{0,8},{8,0},{16,24},{24,16},{1,9},{9,1},{17,25},{25,17},{2,10},{10... | collective-permute-start | bytes 2359304 | tf_op jit(solution)/shard_map/ppermute | solution.py:56
  177.7 32.2 %collective-permute-start.17 = (bf16[256,1536]{1,0:T(8,128)(2,1)S(1)}, bf16[256,1536]{1,0:T(8,128)(2,1)S(1)}, u32[]{:S(2)}, u32[]{:S(2)}) collective-permute-start(bf16[256,1536]{1,0:T(8,128)(2,1)S(1)} %get-tuple-element.27.own), channel_id=1, source_target_pairs={{0,16},{8,24},{16,0},{24,8},{1,17},{9,25},{17,1},{25,9},{2,18},{10... | collective-permute-start | bytes 2359304 | tf_op jit(solution)/shard_map/ppermute | solution.py:56
  178.8 48.4 %collective-permute-start.46 = (bf16[384,512]{1,0:T(8,128)(2,1)S(1)}, bf16[384,512]{1,0:T(8,128)(2,1)S(1)}, u32[]{:S(2)}, u32[]{:S(2)}) collective-permute-start(bf16[384,512]{1,0:T(8,128)(2,1)S(1)} %slice.48), channel_id=1, source_target_pairs={{0,16},{8,24},{16,0},{24,8},{1,17},{9,25},{17,1},{25,9},{2,18},{10... | collective-permute-start | bytes 1179656 | tf_op jit(solution)/shard_map/ppermute | solution.py:56
  185.1 40.6 %collective-permute-start.8 = (bf16[128,1024]{1,0:T(8,128)(2,1)S(1)}, bf16[128,1024]{1,0:T(8,128)(2,1)S(1)}, u32[]{:S(2)}, u32[]{:S(2)}) collective-permute-start(bf16[128,1024]{1,0:T(8,128)(2,1)S(1)} %slice.40), channel_id=1, source_target_pairs={{0,16},{8,24},{16,0},{24,8},{1,17},{9,25},{17,1},{25,9},{2,18},{10... | collective-permute-start | bytes 786440 | tf_op jit(solution)/shard_map/ppermute | solution.py:56
  193.0 33.2 %collective-permute-start.9 = (bf16[128,1024]{1,0:T(8,128)(2,1)S(1)}, bf16[128,1024]{1,0:T(8,128)(2,1)S(1)}, u32[]{:S(2)}, u32[]{:S(2)}) collective-permute-start(bf16[128,1024]{1,0:T(8,128)(2,1)S(1)} %slice.41), channel_id=1, source_target_pairs={{0,8},{8,0},{16,24},{24,16},{1,9},{9,1},{17,25},{25,17},{2,10},{10... | collective-permute-start | bytes 786440 | tf_op jit(solution)/shard_map/ppermute | solution.py:56
  196.3 26.2 %collective-permute-start.42 = (bf16[128,512]{1,0:T(8,128)(2,1)S(1)}, bf16[128,512]{1,0:T(8,128)(2,1)S(1)}, u32[]{:S(2)}, u32[]{:S(2)}) collective-permute-start(bf16[128,512]{1,0:T(8,128)(2,1)S(1)} %slice.46), channel_id=1, source_target_pairs={{0,16},{8,24},{16,0},{24,8},{1,17},{9,25},{17,1},{25,9},{2,18},{10... | collective-permute-start | bytes 393224 | tf_op jit(solution)/shard_map/ppermute | solution.py:56
  209.9 15.1 %collective-permute-start.43 = (bf16[128,512]{1,0:T(8,128)(2,1)S(1)}, bf16[128,512]{1,0:T(8,128)(2,1)}, u32[]{:S(2)}, u32[]{:S(2)}) collective-permute-start(bf16[128,512]{1,0:T(8,128)(2,1)S(1)} %slice.47), channel_id=1, source_target_pairs={{0,8},{8,0},{16,24},{24,16},{1,9},{9,1},{17,25},{25,17},{2,10},{10... | collective-permute-start | bytes 393224 | tf_op jit(solution)/shard_map/ppermute | solution.py:56
  222.5 104.3 %collective-permute-start.47 = (bf16[384,512]{1,0:T(8,128)(2,1)}, bf16[384,512]{1,0:T(8,128)(2,1)S(1)}, u32[]{:S(2)}, u32[]{:S(2)}) collective-permute-start(bf16[384,512]{1,0:T(8,128)(2,1)} %slice.49), channel_id=1, source_target_pairs={{0,8},{8,0},{16,24},{24,16},{1,9},{9,1},{17,25},{25,17},{2,10},{10... | collective-permute-start | bytes 1179656 | tf_op jit(solution)/shard_map/ppermute | solution.py:56
  225.0 199.0 %collective-permute-start.28 = (bf16[128,1536]{1,0:T(8,128)(2,1)}, bf16[128,1536]{1,0:T(8,128)(2,1)S(1)}, u32[]{:S(2)}, u32[]{:S(2)}) collective-permute-start(bf16[128,1536]{1,0:T(8,128)(2,1)} %slice.44), channel_id=1, source_target_pairs={{0,16},{8,24},{16,0},{24,8},{1,17},{9,25},{17,1},{25,9},{2,18},{10... | collective-permute-start | bytes 1179656 | tf_op jit(solution)/shard_map/ppermute | solution.py:56
  225.7 198.3 %collective-permute-start.29 = (bf16[128,1536]{1,0:T(8,128)(2,1)}, bf16[128,1536]{1,0:T(8,128)(2,1)S(1)}, u32[]{:S(2)}, u32[]{:S(2)}) collective-permute-start(bf16[128,1536]{1,0:T(8,128)(2,1)} %slice.45), channel_id=1, source_target_pairs={{0,8},{8,0},{16,24},{24,16},{1,9},{9,1},{17,25},{25,17},{2,10},{10... | collective-permute-start | bytes 1179656 | tf_op jit(solution)/shard_map/ppermute | solution.py:56
  226.3 295.7 %collective-permute-start.18 = (bf16[128,1536]{1,0:T(8,128)(2,1)}, bf16[128,1536]{1,0:T(8,128)(2,1)S(1)}, u32[]{:S(2)}, u32[]{:S(2)}) collective-permute-start(bf16[128,1536]{1,0:T(8,128)(2,1)} %slice.42), channel_id=1, source_target_pairs={{0,16},{8,24},{16,0},{24,8},{1,17},{9,25},{17,1},{25,9},{2,18},{10... | collective-permute-start | bytes 1179656 | tf_op jit(solution)/shard_map/ppermute | solution.py:56
  227.2 294.8 %collective-permute-start.19 = (bf16[128,1536]{1,0:T(8,128)(2,1)S(1)}, bf16[128,1536]{1,0:T(8,128)(2,1)S(1)}, u32[]{:S(2)}, u32[]{:S(2)}) collective-permute-start(bf16[128,1536]{1,0:T(8,128)(2,1)S(1)} %slice.43), channel_id=1, source_target_pairs={{0,8},{8,0},{16,24},{24,16},{1,9},{9,1},{17,25},{25,17},{2,10},{10... | collective-permute-start | bytes 1179656 | tf_op jit(solution)/shard_map/ppermute | solution.py:56
  (43 other events, 950.5 us)

commit v2 on v1

--- a/solution.py
+++ b/solution.py
@@ -63,8 +63,9 @@
     def block(owner):
         return lax.dynamic_slice(matrix, (low, owner * width), (rows, width))
 
-    far = swap(encode(block(me ^ 3), inner_limit), first, "rep")
-    near = swap(encode(block(me ^ first), inner_limit), first, "rep")
+    sent = encode(jnp.concatenate([block(me ^ 3), block(me ^ first)], axis=0), inner_limit)
+    came = swap(sent, first, "rep")
+    far, near = came[:rows], came[rows:]
     relay = block(me ^ second) + decode(far, inner_limit)
     across = swap(encode(relay, 2 * inner_limit), second, "rep")
     return block(me) + decode(near, inner_limit) + decode(across, 2 * inner_limit)
@@ -83,46 +84,70 @@
     )
 
 
-def place_kernel(own, by_x, by_y, far_top, far_low, out, sems):
-    me = lax.axis_index("rep")
-    rows, width = own.shape
-    half = rows // 2
-
-    def columns(owner):
-        return pl.ds(pl.multiple_of(owner * width, 128), width)
-
-    copies = [
-        pltpu.make_async_copy(own, out.at[:, columns(me)], sems.at[0]),
-        pltpu.make_async_copy(by_x, out.at[:, columns(me ^ 1)], sems.at[1]),
-        pltpu.make_async_copy(by_y, out.at[:, columns(me ^ 2)], sems.at[2]),
-        pltpu.make_async_copy(far_top, out.at[pl.ds(0, half), columns(me ^ 3)], sems.at[3]),
-        pltpu.make_async_copy(far_low, out.at[pl.ds(half, half), columns(me ^ 3)], sems.at[4]),
-    ]
-    for copy in copies:
-        copy.start()
-    for copy in copies:
-        copy.wait()
-
-
-def gather_columns(own):
-    if lax.axis_size("rep") != 4:
-        return lax.all_gather(own, "rep", axis=1, tiled=True)
-    rows, width = own.shape
-    half = rows // 2
-    by_x = swap(own, 1, "rep")
-    by_y = swap(own, 2, "rep")
-    far_top = swap(by_x[:half], 2, "rep")
-    far_low = swap(by_y[half:], 1, "rep")
+def place(pieces, low, rows):
+    own = pieces[0]
+    width = own.shape[1]
+    half = own.shape[0] // 2
+    tile = math.gcd(math.gcd(half, 128), math.gcd(low, rows))
+    start, middle = low // tile, half // tile
+
+    def body(own, by_x, by_y, far_top, far_low, out):
+        me = lax.axis_index("rep")
+
+        def columns(owner):
+            return pl.ds(pl.multiple_of(owner * width, 128), width)
+
+        out[:, columns(me)] = own[...]
+        out[:, columns(me ^ 1)] = by_x[...]
+        out[:, columns(me ^ 2)] = by_y[...]
+        is_top = pl.program_id(0) + start < middle
+
+        @pl.when(is_top)
+        def _():
+            out[:, columns(me ^ 3)] = far_top[...]
+
+        @pl.when(jnp.logical_not(is_top))
+        def _():
+            out[:, columns(me ^ 3)] = far_low[...]
+
+    def whole(i):
+        return (i + start, 0)
+
+    def upper(i):
+        return (jnp.minimum(i + start, middle - 1), 0)
+
+    def lower(i):
+        return (jnp.maximum(i + start - middle, 0), 0)
+
     return pl.pallas_call(
-        place_kernel,
+        body,
+        grid=(rows // tile,),
         out_shape=jax.ShapeDtypeStruct((rows, 4 * width), own.dtype),
-        in_specs=[pl.BlockSpec(memory_space=pl.ANY)] * 5,
-        out_specs=pl.BlockSpec(memory_space=pl.ANY),
-        scratch_shapes=[pltpu.SemaphoreType.DMA((5,))],
+        in_specs=[pl.BlockSpec((tile, width), m) for m in (whole, whole, whole, upper, lower)],
+        out_specs=pl.BlockSpec((tile, 4 * width), lambda i: (i, 0)),
+        compiler_params=pltpu.CompilerParams(vmem_limit_bytes=16 * 2**20),
         cost_estimate=pl.CostEstimate(
             flops=0, bytes_accessed=16 * rows * width, transcendentals=0
         ),
-    )(own, by_x, by_y, far_top, far_low)
+    )(*pieces)
+
+
+def exchange(own):
+    half = own.shape[0] // 2
+    by_x = swap(own, 1, "rep")
+    by_y = swap(own, 2, "rep")
+    return own, by_x, by_y, swap(by_x[:half], 2, "rep"), swap(by_y[half:], 1, "rep")
+
+
+def gather_columns(*parts):
+    if lax.axis_size("rep") != 4:
+        return [lax.all_gather(part, "rep", axis=1, tiled=True) for part in parts]
+    pieces = exchange(jnp.concatenate(parts, axis=0) if len(parts) > 1 else parts[0])
+    fresh, low = [], 0
+    for part in parts:
+        fresh.append(place(pieces, low, part.shape[0]))
+        low += part.shape[0]
+    return fresh
 
 
 def coefficients(inner_out, inner_down, outer_out, outer_down, basis_out, basis_down):
@@ -185,12 +210,16 @@
     a3, b3, c3 = nesterov(outer_w3, moment_w3, d_three)
     ao, bo, co = nesterov(outer_wo, moment_wo, d_out)
     a2, b2, c2 = nesterov(outer_w2, moment_w2, d_down)
+    (w0,) = gather_columns(a0)
+    wo, w2 = gather_columns(ao, a2)
+    (w1,) = gather_columns(a1)
+    (w3,) = gather_columns(a3)
     return (
-        gather_columns(a0),
-        gather_columns(a1),
-        gather_columns(a3),
-        gather_columns(ao),
-        gather_columns(a2),
+        w0,
+        w1,
+        w3,
+        wo,
+        w2,
         b0,
         b1,
         b3,

time: 620 us -> 227 us (0.37)
  Pallas kernels: 387 us -> 8.7 us
  starting transfers between devices: 56.8 us -> 40.1 us
    pallas_call x5, Pallas kernels: 387 us -> 8.7 us  [place(): pl.pallas_call(body, grid=(rows // tile,), out_shape=jax.ShapeDtypeStruct...]
    ppermute x48 -> x36, starting transfers between devices: 56.8 us -> 40.1 us  [swap(): lax.ppermute(value, axis, [(i, i ^ bit) for i in range(lax.axis_size(axis...]
    ppermute x48 -> x36, waiting for transfers between devices: 121 us -> 125 us  [swap(): lax.ppermute(value, axis, [(i, i ^ bit) for i in range(lax.axis_size(axis...]
  transfers between devices with their start and end apart: 48 -> 36, of which waited for: 17 -> 14; matrix products, arithmetic and copies ran while one was open for 7% -> 21% of each run, Pallas kernels for 47% -> 2%
where the time goes in v2:
time: 227 us; the launch traced here: 226 us
  waiting for transfers between devices  125 us (55%)
  starting transfers between devices  40.1 us (18%)
  other arithmetic  27.6 us (12%)
  matrix products  15.3 us (7%)
  Pallas kernels  8.7 us (4%)
  local copies, waits for them, and re-layouts  8.69 us (4%)
    ppermute x36, waiting for transfers between devices, swap(): lax.ppermute(value, axis, [(i, i ^ bit) for i in range(lax.axis_size(axis...  125 us
    ppermute x36, starting transfers between devices, swap(): lax.ppermute(value, axis, [(i, i ^ bit) for i in range(lax.axis_size(axis...  40.1 us
    convert_element_type x9, other arithmetic, pack(): return jnp.where(value < 0, -size, size).astype(jnp.bfloat16)  11.7 us
    dot_general x4, matrix products, project(): lax.dot_general(basis, matrix, (((0,), (0,)), ((), ())), precision=lax.Pr...  9.88 us
    pallas_call x5, Pallas kernels, place(): pl.pallas_call(body, grid=(rows // tile,), out_shape=jax.ShapeDtypeStruct...  8.7 us
    dynamic_slice x5, local copies, waits for them, and re-layouts, block(): return lax.dynamic_slice(matrix, (low, owner * width), (rows, width))  6.78 us
    convert_element_type x3, other arithmetic, nesterov(): return (master.astype(jnp.bfloat16), master, moment_new)  6.23 us
    dot_general x2, matrix products, rebuild(): jnp.dot(basis, coeff, precision=lax.Precision.HIGHEST, preferred_element_...  5.38 us
  transfers between devices with their start and end apart: 36, of which 14 were waited for; matrix products, arithmetic and copies ran while one was open for 21% of the time, Pallas kernels for 2%

profile of v2, /device:TPU:0, one launch (start us, length us, event | category | flops | bytes accessed | tf_op | source)
XLA Modules:
  0.0 226.2 jit_solution(17930734018198093545)
XLA Ops:
  0.7 1.6 copy-done
  2.2 2.3 fusion.2
  5.3 2.9 %collective-permute-start.24 = (f32[128,512]{1,0:T(8,128)}, f32[128,512]{1,0:T(8,128)}, u32[]{:S(2)}, u32[]{:S(2)}) collective-permute-start(f32[128,512]{1,0:T(8,128)} %pad_maximum_fusion.7), channel_id=1, source_target_pairs={{0,8},{8,0},{16,24},{24,16},{1,9},{9,1},{17,25},{25,17},{2,10},{10... | collective-permute-start | bytes 786440 | tf_op jit(solution)/shard_map/ppermute | solution.py:56
  8.2 6.1 %fusion = f32[64,2048]{1,0:T(8,128)S(1)} fusion(f32[768,64]{0,1:T(8,128)S(1)} %copy-done.8, f32[1,768,2048]{2,1,0:T(8,128)} %param.21), kind=kOutput, calls=%fused_computation | convolution fusion | flops 1207959552 | bytes 7012352 | tf_op jit(solution)/shard_map/dot_general | solution.py:17
  15.2 1.5 collective-permute-start.26
  16.7 2.9 %dynamic-slice_bitcast_fusion.7 = (f32[128,1536]{1,0:T(8,128)S(1)}, f32[128,1536]{1,0:T(8,128)S(1)}, f32[128,1536]{1,0:T(8,128)}, f32[128,1536]{1,0:T(8,128)S(1)}) fusion(f32[1,256,6144]{2,1,0:T(8,128)} %param.18, s32[]{:T(128)S(6)} %select_n.192, s32[]{:T(128)S(6)} %select_n.193, s32[]{:T(128)S(6)} %select_n.196), kind=kLoop, calls=%fused_computation.139 | loop fusion | bytes 6291468 | tf_op jit(solution)/shard_map/dynamic_slice | solution.py:64
  21.5 1.7 dynamic-slice_bitcast_fusion.11
  24.3 1.5 collective-permute-start.2
  28.5 2.1 dynamic-slice_bitcast_fusion.3
  35.3 2.0 collective-permute-start.27
  37.7 16.3 %collective-permute-done.25 = f32[64,512]{1,0:T(8,128)S(1)} collective-permute-done((f32[64,512]{1,0:T(8,128)S(1)}, f32[64,512]{1,0:T(8,128)S(1)}, u32[]{:S(2)}, u32[]{:S(2)}) %collective-permute-start.25) | collective-permute-done | bytes 131104 | tf_op jit(solution)/shard_map/ppermute | solution.py:56
  55.7 2.2 fusion.88
  57.8 1.7 collective-permute-start.1
  59.5 1.5 collective-permute-start.3
  61.1 1.6 collective-permute-start.29
  63.2 3.3 %collective-permute-done.29 = f32[64,512]{1,0:T(8,128)S(1)} collective-permute-done((f32[64,512]{1,0:T(8,128)S(1)}, f32[64,512]{1,0:T(8,128)S(1)}, u32[]{:S(2)}, u32[]{:S(2)}) %collective-permute-start.29) | collective-permute-done | bytes 131104 | tf_op jit(solution)/shard_map/ppermute | solution.py:56
  68.2 12.1 %collective-permute-done.3 = bf16[128,1024]{1,0:T(8,128)(2,1)S(1)} collective-permute-done((bf16[128,1024]{1,0:T(8,128)(2,1)S(1)}, bf16[128,1024]{1,0:T(8,128)(2,1)S(1)}, u32[]{:S(2)}, u32[]{:S(2)}) %collective-permute-start.3) | collective-permute-done | bytes 262176 | tf_op jit(solution)/shard_map/ppermute | solution.py:56
  80.4 2.6 %collective-permute-start.30 = (f32[64,512]{1,0:T(8,128)S(1)}, f32[64,512]{1,0:T(8,128)S(1)}, u32[]{:S(2)}, u32[]{:S(2)}) collective-permute-start(f32[64,512]{1,0:T(8,128)S(1)} %add.299), channel_id=1, source_target_pairs={{0,4},{1,5},{2,6},{3,7},{4,0},{5,1},{6,2},{7,3},{8,12},{9,13},{10,... | collective-permute-start | bytes 393224 | tf_op jit(solution)/shard_map/ppermute | solution.py:56
  83.0 2.0 fusion.86
  85.0 1.7 fusion.111
  88.2 2.0 fusion.54
  90.2 1.7 collective-permute-start.11
  91.9 5.4 %collective-permute-done.16 = bf16[256,1536]{1,0:T(8,128)(2,1)S(1)} collective-permute-done((bf16[256,1536]{1,0:T(8,128)(2,1)S(1)}, bf16[256,1536]{1,0:T(8,128)(2,1)S(1)}, u32[]{:S(2)}, u32[]{:S(2)}) %collective-permute-start.16) | collective-permute-done | bytes 786464 | tf_op jit(solution)/shard_map/ppermute | solution.py:56
  98.2 1.6 collective-permute-start.17
  100.7 1.7 fusion.104
  102.5 3.7 %fusion.105 = (bf16[768,512]{1,0:T(8,128)(2,1)S(1)}, f32[768,512]{1,0:T(8,128)}, f32[768,512]{1,0:T(8,128)}) fusion(f32[768,512]{1,0:T(8,128)S(1)} %copy-done.3, f32[768,512]{1,0:T(8,128)S(1)} %copy-done.11, f32[768,64]{0,1:T(8,128)S(1)} %copy-done.10, f32[64,512]{1,0:T(8,128)S(1)} %collective-permute-done.31, f32[64,512]{1,0:T(8,128)S(1)} %add.300, ...), kind=kOutput, calls=%fused_computation.216 | convolution fusion | flops 304775168 | bytes 7536641 | tf_op jit(solution)/shard_map/dot_general | solution.py:27
  106.1 10.7 %collective-permute-done.11 = bf16[128,1536]{1,0:T(8,128)(2,1)S(1)} collective-permute-done((bf16[128,1536]{1,0:T(8,128)(2,1)S(1)}, bf16[128,1536]{1,0:T(8,128)(2,1)S(1)}, u32[]{:S(2)}, u32[]{:S(2)}) %collective-permute-start.11) | collective-permute-done | bytes 393248 | tf_op jit(solution)/shard_map/ppermute | solution.py:56
  116.9 1.5 collective-permute-start.5
  118.4 4.5 %collective-permute-done.19 = bf16[128,1536]{1,0:T(8,128)(2,1)S(1)} collective-permute-done((bf16[128,1536]{1,0:T(8,128)(2,1)S(1)}, bf16[128,1536]{1,0:T(8,128)(2,1)S(1)}, u32[]{:S(2)}, u32[]{:S(2)}) %collective-permute-start.19) | collective-permute-done | bytes 393248 | tf_op jit(solution)/shard_map/ppermute | solution.py:56
  122.9 3.1 %fusion.52 = (f32[128,1536]{1,0:T(8,128)S(1)}, f32[128,1536]{1,0:T(8,128)S(1)}, f32[128,1536]{1,0:T(8,128)S(1)}, f32[128,1536]{1,0:T(8,128)S(1)}) fusion(bf16[128,1536]{1,0:T(8,128)(2,1)S(1)} %collective-permute-done.9, f32[1,256,6144]{2,1,0:T(8,128)S(1)} %bitcast.86, s32[]{:T(128)S(6)} %select_n.191, bf16[256,1536]{1,0:T(8,128)(2,1)S(1)} %collective-permute-done.8, ...), kind=kLoop, calls=%fused_computation.117 | loop fusion | flops 12582912 | bytes 9437188 | tf_op jit(solution)/shard_map/add | solution.py:71
  125.9 2.3 %fusion.109 = (bf16[256,1536]{1,0:T(8,128)(2,1)S(1)}, f32[256,1536]{1,0:T(8,128)}, f32[256,1536]{1,0:T(8,128)}) fusion(f32[256,1536]{1,0:T(8,128)S(1)} %copy-done.12, f32[128,1536]{1,0:T(8,128)S(1)} %get-tuple-element.61, f32[128,1536]{1,0:T(8,128)S(1)} %get-tuple-element.62, f32[256,1536]{1,0:T(8,128)S(1)} %copy-done.13), kind=kLoop, calls=%fused_computation.217 | loop fusion | flops 3932160 | bytes 8650752 | tf_op jit(solution)/shard_map/convert_element_type | solution.py:35
  128.6 1.8 collective-permute-start.32
  130.4 2.0 collective-permute-start.33
  132.4 2.3 %fusion.110 = (bf16[256,1536]{1,0:T(8,128)(2,1)S(1)}, f32[256,1536]{1,0:T(8,128)}, f32[256,1536]{1,0:T(8,128)}) fusion(f32[256,1536]{1,0:T(8,128)S(1)} %copy-done.14, f32[128,1536]{1,0:T(8,128)S(1)} %get-tuple-element.42, f32[128,1536]{1,0:T(8,128)S(1)} %get-tuple-element.41, f32[256,1536]{1,0:T(8,128)S(1)} %copy-done.15), kind=kLoop, calls=%fused_computation.218 | loop fusion | flops 3932160 | bytes 8650752 | tf_op jit(solution)/shard_map/convert_element_type | solution.py:35
  135.0 13.7 %collective-permute-done.20.by_x = bf16[256,1536]{1,0:T(8,128)(2,1)S(1)} collective-permute-done((bf16[256,1536]{1,0:T(8,128)(2,1)S(1)}, bf16[256,1536]{1,0:T(8,128)(2,1)S(1)}, u32[]{:S(2)}, u32[]{:S(2)}) %collective-permute-start.20) | collective-permute-done | bytes 786464 | tf_op jit(solution)/shard_map/ppermute | solution.py:56
  148.7 2.0 collective-permute-start.13
  150.7 20.5 %collective-permute-done.32.by_x = bf16[1024,512]{1,0:T(8,128)(2,1)S(1)} collective-permute-done((bf16[1024,512]{1,0:T(8,128)(2,1)S(1)}, bf16[1024,512]{1,0:T(8,128)(2,1)S(1)}, u32[]{:S(2)}, u32[]{:S(2)}) %collective-permute-start.32) | collective-permute-done | bytes 1048608 | tf_op jit(solution)/shard_map/ppermute | solution.py:56
  171.2 2.0 collective-permute-start.22
  173.8 14.2 %collective-permute-done.12.by_x = bf16[256,1536]{1,0:T(8,128)(2,1)S(1)} collective-permute-done((bf16[256,1536]{1,0:T(8,128)(2,1)S(1)}, bf16[256,1536]{1,0:T(8,128)(2,1)S(1)}, u32[]{:S(2)}, u32[]{:S(2)}) %collective-permute-start.12) | collective-permute-done | bytes 786464 | tf_op jit(solution)/shard_map/ppermute | solution.py:56
  188.0 2.0 collective-permute-start.34
  190.6 13.7 %collective-permute-done.6.far_top = bf16[128,1024]{1,0:T(8,128)(2,1)S(1)} collective-permute-done((bf16[128,1024]{1,0:T(8,128)(2,1)S(1)}, bf16[128,1024]{1,0:T(8,128)(2,1)S(1)}, u32[]{:S(2)}, u32[]{:S(2)}) %collective-permute-start.6) | collective-permute-done | bytes 262176 | tf_op jit(solution)/shard_map/ppermute | solution.py:56
  204.5 2.0 collective-permute-start.14
  206.5 1.7 collective-permute-start.15
  209.6 4.5 %collective-permute-done.23.far_low = bf16[128,1536]{1,0:T(8,128)(2,1)S(1)} collective-permute-done((bf16[128,1536]{1,0:T(8,128)(2,1)S(1)}, bf16[128,1536]{1,0:T(8,128)(2,1)S(1)}, u32[]{:S(2)}, u32[]{:S(2)}) %collective-permute-start.23) | collective-permute-done | bytes 393248 | tf_op jit(solution)/shard_map/ppermute | solution.py:56
  214.1 1.8 shard_map.282
  215.9 4.7 %collective-permute-done.14.far_top = bf16[128,1536]{1,0:T(8,128)(2,1)S(1)} collective-permute-done((bf16[128,1536]{1,0:T(8,128)(2,1)S(1)}, bf16[128,1536]{1,0:T(8,128)(2,1)S(1)}, u32[]{:S(2)}, u32[]{:S(2)}) %collective-permute-start.14) | collective-permute-done | bytes 393248 | tf_op jit(solution)/shard_map/ppermute | solution.py:56
  220.7 1.8 shard_map.281
  222.4 2.7 %shard_map.284 = bf16[768,2048]{1,0:T(8,128)(2,1)} custom-call(bf16[1024,512]{1,0:T(8,128)(2,1)S(1)} %pad_maximum_fusion.6.own, bf16[1024,512]{1,0:T(8,128)(2,1)S(1)} %collective-permute-done.32.by_x, bf16[1024,512]{1,0:T(8,128)(2,1)S(1)} %collective-permute-done.33.by_y, bf16[512,512]{1,0:T(8,128)(2,1)S(1)} %collective-permute-done.34.far_top, ...), custom_call_target="tpu_custom_call" | custom-call | bytes 6291456 | tf_op jit(solution)/shard_map/pallas_call | solution.py:122
  (123 shorter events, 24.0 us)
Async XLA Ops:
  2.2 6.0 %copy-start.8 = (f32[768,64]{0,1:T(8,128)S(1)}, f32[768,64]{0,1:T(8,128)}, u32[]{:S(2)}) copy-start(f32[768,64]{0,1:T(8,128)} %param.33) | copy-start | bytes 589828
  5.3 28.0 %collective-permute-start.24 = (f32[128,512]{1,0:T(8,128)}, f32[128,512]{1,0:T(8,128)}, u32[]{:S(2)}, u32[]{:S(2)}) collective-permute-start(f32[128,512]{1,0:T(8,128)} %pad_maximum_fusion.7), channel_id=1, source_target_pairs={{0,8},{8,0},{16,24},{24,16},{1,9},{9,1},{17,25},{25,17},{2,10},{10... | collective-permute-start | bytes 786440 | tf_op jit(solution)/shard_map/ppermute | solution.py:56
  15.2 19.1 %collective-permute-start.26 = (f32[128,512]{1,0:T(8,128)}, f32[128,512]{1,0:T(8,128)}, u32[]{:S(2)}, u32[]{:S(2)}) collective-permute-start(f32[128,512]{1,0:T(8,128)} %pad_maximum_fusion.8), channel_id=1, source_target_pairs={{0,16},{8,24},{16,0},{24,8},{1,17},{9,25},{17,1},{25,9},{2,18},{10... | collective-permute-start | bytes 786440 | tf_op jit(solution)/shard_map/ppermute | solution.py:56
  21.0 67.1 %collective-permute-start.10 = (bf16[256,1536]{1,0:T(8,128)(2,1)}, bf16[256,1536]{1,0:T(8,128)(2,1)}, u32[]{:S(2)}, u32[]{:S(2)}) collective-permute-start(bf16[256,1536]{1,0:T(8,128)(2,1)} %fusion.5), channel_id=1, source_target_pairs={{0,16},{8,24},{16,0},{24,8},{1,17},{9,25},{17,1},{25,9},{2,18},{10... | collective-permute-start | bytes 2359304 | tf_op jit(solution)/shard_map/ppermute | solution.py:56
  24.3 31.4 %collective-permute-start.2 = (bf16[256,1024]{1,0:T(8,128)(2,1)}, bf16[256,1024]{1,0:T(8,128)(2,1)}, u32[]{:S(2)}, u32[]{:S(2)}) collective-permute-start(bf16[256,1024]{1,0:T(8,128)(2,1)} %fusion.13), channel_id=1, source_target_pairs={{0,16},{8,24},{16,0},{24,8},{1,17},{9,25},{17,1},{25,9},{2,18},{10... | collective-permute-start | bytes 1572872 | tf_op jit(solution)/shard_map/ppermute | solution.py:56
  26.9 28.8 %collective-permute-start = (bf16[256,1024]{1,0:T(8,128)(2,1)}, bf16[256,1024]{1,0:T(8,128)(2,1)}, u32[]{:S(2)}, u32[]{:S(2)}) collective-permute-start(bf16[256,1024]{1,0:T(8,128)(2,1)} %fusion.12), channel_id=1, source_target_pairs={{0,8},{8,0},{16,24},{24,16},{1,9},{9,1},{17,25},{25,17},{2,10},{10... | collective-permute-start | bytes 1572872 | tf_op jit(solution)/shard_map/ppermute | solution.py:56
  34.2 19.8 %collective-permute-start.25 = (f32[64,512]{1,0:T(8,128)S(1)}, f32[64,512]{1,0:T(8,128)S(1)}, u32[]{:S(2)}, u32[]{:S(2)}) collective-permute-start(f32[64,512]{1,0:T(8,128)S(1)} %slice_add_fusion.2), channel_id=1, source_target_pairs={{0,16},{8,24},{16,0},{24,8},{1,17},{9,25},{17,1},{25,9},{2,18},{10... | collective-permute-start | bytes 393224 | tf_op jit(solution)/shard_map/ppermute | solution.py:56
  35.3 19.2 %collective-permute-start.27 = (f32[64,512]{1,0:T(8,128)S(1)}, f32[64,512]{1,0:T(8,128)S(1)}, u32[]{:S(2)}, u32[]{:S(2)}) collective-permute-start(f32[64,512]{1,0:T(8,128)S(1)} %slice_add_fusion), channel_id=1, source_target_pairs={{0,8},{8,0},{16,24},{24,16},{1,9},{9,1},{17,25},{25,17},{2,10},{10... | collective-permute-start | bytes 393224 | tf_op jit(solution)/shard_map/ppermute | solution.py:56
  54.1 34.1 %collective-permute-start.8 = (bf16[256,1536]{1,0:T(8,128)(2,1)}, bf16[256,1536]{1,0:T(8,128)(2,1)S(1)}, u32[]{:S(2)}, u32[]{:S(2)}) collective-permute-start(bf16[256,1536]{1,0:T(8,128)(2,1)} %fusion.4), channel_id=1, source_target_pairs={{0,8},{8,0},{16,24},{24,16},{1,9},{9,1},{17,25},{25,17},{2,10},{10... | collective-permute-start | bytes 2359304 | tf_op jit(solution)/shard_map/ppermute | solution.py:56
  55.5 5.5 %collective-permute-start.28 = (f32[64,512]{1,0:T(8,128)S(1)}, f32[64,512]{1,0:T(8,128)S(1)}, u32[]{:S(2)}, u32[]{:S(2)}) collective-permute-start(f32[64,512]{1,0:T(8,128)S(1)} %get-tuple-element.21), channel_id=1, source_target_pairs={{0,1},{1,0},{2,3},{3,2},{4,5},{5,4},{6,7},{7,6},{8,9},{9,8},{10,11... | collective-permute-start | bytes 393224 | tf_op jit(solution)/shard_map/ppermute | solution.py:56
  55.6 32.5 %slice-start = ((s8[6291456]{0:T(1024)(128)(4,1)}), s8[4194304]{0:T(1024)(128)(4,1)S(1)}, s32[]{:S(2)}) async-start(s8[6291456]{0:T(1024)(128)(4,1)} %bitcast.85), calls=%async_computation | async-start | bytes 8388608
  57.8 8.6 %copy-start.18 = (bf16[256,1536]{1,0:T(8,128)(2,1)S(1)}, bf16[256,1536]{1,0:T(8,128)(2,1)}, u32[]{:S(2)}) copy-start(bf16[256,1536]{1,0:T(8,128)(2,1)} %fusion.6) | copy-start | bytes 2359300
  57.8 9.2 %collective-permute-start.1 = (bf16[128,1024]{1,0:T(8,128)(2,1)S(1)}, bf16[128,1024]{1,0:T(8,128)(2,1)S(1)}, u32[]{:S(2)}, u32[]{:S(2)}) collective-permute-start(bf16[128,1024]{1,0:T(8,128)(2,1)S(1)} %get-tuple-element.51), channel_id=1, source_target_pairs={{0,16},{8,24},{16,0},{24,8},{1,17},{9,25},{17,1},{25,9},{2,18},{10... | collective-permute-start | bytes 786440 | tf_op jit(solution)/shard_map/ppermute | solution.py:56
  59.5 20.8 %collective-permute-start.3 = (bf16[128,1024]{1,0:T(8,128)(2,1)S(1)}, bf16[128,1024]{1,0:T(8,128)(2,1)S(1)}, u32[]{:S(2)}, u32[]{:S(2)}) collective-permute-start(bf16[128,1024]{1,0:T(8,128)(2,1)S(1)} %get-tuple-element.52), channel_id=1, source_target_pairs={{0,8},{8,0},{16,24},{24,16},{1,9},{9,1},{17,25},{25,17},{2,10},{10... | collective-permute-start | bytes 786440 | tf_op jit(solution)/shard_map/ppermute | solution.py:56
  61.0 24.0 %copy-start.16 = (f32[256,1024]{1,0:T(8,128)S(1)}, f32[256,1024]{1,0:T(8,128)}, u32[]{:S(2)}) copy-start(f32[256,1024]{1,0:T(8,128)} %param.22) | copy-start | bytes 3145732
  61.0 24.0 %copy-start.17 = (f32[256,1024]{1,0:T(8,128)S(1)}, f32[256,1024]{1,0:T(8,128)}, u32[]{:S(2)}) copy-start(f32[256,1024]{1,0:T(8,128)} %param.27) | copy-start | bytes 3145732
  61.1 5.4 %collective-permute-start.29 = (f32[64,512]{1,0:T(8,128)S(1)}, f32[64,512]{1,0:T(8,128)S(1)}, u32[]{:S(2)}, u32[]{:S(2)}) collective-permute-start(f32[64,512]{1,0:T(8,128)S(1)} %select_add_fusion), channel_id=1, source_target_pairs={{0,2},{1,3},{2,0},{3,1},{4,6},{5,7},{6,4},{7,5},{8,10},{9,11},{10,... | collective-permute-start | bytes 393224 | tf_op jit(solution)/shard_map/ppermute | solution.py:56
  62.7 34.5 %slice-start.2 = ((s8[6291456]{0:T(1024)(128)(4,1)}), s8[4194304]{0:T(1024)(128)(4,1)S(1)}, s32[]{:S(2)}) async-start(s8[6291456]{0:T(1024)(128)(4,1)} %bitcast.87), calls=%async_computation.2 | async-start | bytes 8388608
  66.4 30.8 %collective-permute-start.16 = (bf16[256,1536]{1,0:T(8,128)(2,1)S(1)}, bf16[256,1536]{1,0:T(8,128)(2,1)S(1)}, u32[]{:S(2)}, u32[]{:S(2)}) collective-permute-start(bf16[256,1536]{1,0:T(8,128)(2,1)S(1)} %copy-done.18), channel_id=1, source_target_pairs={{0,8},{8,0},{16,24},{24,16},{1,9},{9,1},{17,25},{25,17},{2,10},{10... | collective-permute-start | bytes 2359304 | tf_op jit(solution)/shard_map/ppermute | solution.py:56
  67.0 21.2 %slice-start.1 = ((s8[6291456]{0:T(1024)(128)(4,1)}), s8[2097152]{0:T(1024)(128)(4,1)S(1)}, s32[]{:S(2)}) async-start(s8[6291456]{0:T(1024)(128)(4,1)} %bitcast.85), calls=%async_computation.1 | async-start | bytes 4194304
  67.0 30.2 %collective-permute-start.18 = (bf16[256,1536]{1,0:T(8,128)(2,1)S(1)}, bf16[256,1536]{1,0:T(8,128)(2,1)S(1)}, u32[]{:S(2)}, u32[]{:S(2)}) collective-permute-start(bf16[256,1536]{1,0:T(8,128)(2,1)S(1)} %fusion.7), channel_id=1, source_target_pairs={{0,16},{8,24},{16,0},{24,8},{1,17},{9,25},{17,1},{25,9},{2,18},{10... | collective-permute-start | bytes 2359304 | tf_op jit(solution)/shard_map/ppermute | solution.py:56
  80.4 7.3 %collective-permute-start.30 = (f32[64,512]{1,0:T(8,128)S(1)}, f32[64,512]{1,0:T(8,128)S(1)}, u32[]{:S(2)}, u32[]{:S(2)}) collective-permute-start(f32[64,512]{1,0:T(8,128)S(1)} %add.299), channel_id=1, source_target_pairs={{0,4},{1,5},{2,6},{3,7},{4,0},{5,1},{6,2},{7,3},{8,12},{9,13},{10,... | collective-permute-start | bytes 393224 | tf_op jit(solution)/shard_map/ppermute | solution.py:56
  85.0 12.2 %slice-start.3 = ((s8[6291456]{0:T(1024)(128)(4,1)}), s8[2097152]{0:T(1024)(128)(4,1)S(1)}, s32[]{:S(2)}) async-start(s8[6291456]{0:T(1024)(128)(4,1)} %bitcast.87), calls=%async_computation.3 | async-start | bytes 4194304
  87.6 44.7 %collective-permute-start.4 = (bf16[256,1024]{1,0:T(8,128)(2,1)S(1)}, bf16[256,1024]{1,0:T(8,128)(2,1)S(1)}, u32[]{:S(2)}, u32[]{:S(2)}) collective-permute-start(bf16[256,1024]{1,0:T(8,128)(2,1)S(1)} %get-tuple-element.30.own), channel_id=1, source_target_pairs={{0,8},{8,0},{16,24},{24,16},{1,9},{9,1},{17,25},{25,17},{2,10},{10... | collective-permute-start | bytes 1572872 | tf_op jit(solution)/shard_map/ppermute | solution.py:56
  88.1 12.3 %collective-permute-start.31 = (f32[64,512]{1,0:T(8,128)S(1)}, f32[64,512]{1,0:T(8,128)S(1)}, u32[]{:S(2)}, u32[]{:S(2)}) collective-permute-start(f32[64,512]{1,0:T(8,128)S(1)} %add.300), channel_id=1, source_target_pairs={{0,1},{1,0},{2,3},{3,2},{4,5},{5,4},{6,7},{7,6},{8,9},{9,8},{10,11... | collective-permute-start | bytes 393224 | tf_op jit(solution)/shard_map/ppermute | solution.py:56
  90.2 10.6 %copy-start.20 = (f32[256,512]{1,0:T(8,128)S(1)}, f32[256,512]{1,0:T(8,128)}, u32[]{:S(2)}) copy-start(f32[256,512]{1,0:T(8,128)} %param.30) | copy-start | bytes 1572868
  90.2 26.7 %collective-permute-start.11 = (bf16[128,1536]{1,0:T(8,128)(2,1)S(1)}, bf16[128,1536]{1,0:T(8,128)(2,1)S(1)}, u32[]{:S(2)}, u32[]{:S(2)}) collective-permute-start(bf16[128,1536]{1,0:T(8,128)(2,1)S(1)} %get-tuple-element.44), channel_id=1, source_target_pairs={{0,8},{8,0},{16,24},{24,16},{1,9},{9,1},{17,25},{25,17},{2,10},{10... | collective-permute-start | bytes 1179656 | tf_op jit(solution)/shard_map/ppermute | solution.py:56
  98.2 20.2 %collective-permute-start.17 = (bf16[128,1536]{1,0:T(8,128)(2,1)S(1)}, bf16[128,1536]{1,0:T(8,128)(2,1)S(1)}, u32[]{:S(2)}, u32[]{:S(2)}) collective-permute-start(bf16[128,1536]{1,0:T(8,128)(2,1)S(1)} %get-tuple-element.35), channel_id=1, source_target_pairs={{0,16},{8,24},{16,0},{24,8},{1,17},{9,25},{17,1},{25,9},{2,18},{10... | collective-permute-start | bytes 1179656 | tf_op jit(solution)/shard_map/ppermute | solution.py:56
  99.8 23.0 %collective-permute-start.19 = (bf16[128,1536]{1,0:T(8,128)(2,1)S(1)}, bf16[128,1536]{1,0:T(8,128)(2,1)S(1)}, u32[]{:S(2)}, u32[]{:S(2)}) collective-permute-start(bf16[128,1536]{1,0:T(8,128)(2,1)S(1)} %get-tuple-element.36), channel_id=1, source_target_pairs={{0,8},{8,0},{16,24},{24,16},{1,9},{9,1},{17,25},{25,17},{2,10},{10... | collective-permute-start | bytes 1179656 | tf_op jit(solution)/shard_map/ppermute | solution.py:56
  100.4 22.5 %collective-permute-start.9 = (bf16[128,1536]{1,0:T(8,128)(2,1)S(1)}, bf16[128,1536]{1,0:T(8,128)(2,1)S(1)}, u32[]{:S(2)}, u32[]{:S(2)}) collective-permute-start(bf16[128,1536]{1,0:T(8,128)(2,1)S(1)} %get-tuple-element.43), channel_id=1, source_target_pairs={{0,16},{8,24},{16,0},{24,8},{1,17},{9,25},{17,1},{25,9},{2,18},{10... | collective-permute-start | bytes 1179656 | tf_op jit(solution)/shard_map/ppermute | solution.py:56
  106.1 19.8 %copy-start.12 = (f32[256,1536]{1,0:T(8,128)S(1)}, f32[256,1536]{1,0:T(8,128)}, u32[]{:S(2)}) copy-start(f32[256,1536]{1,0:T(8,128)} %param.24) | copy-start | bytes 4718596
  106.1 19.8 %copy-start.13 = (f32[256,1536]{1,0:T(8,128)S(1)}, f32[256,1536]{1,0:T(8,128)}, u32[]{:S(2)}) copy-start(f32[256,1536]{1,0:T(8,128)} %param.29) | copy-start | bytes 4718596
  116.9 17.8 %collective-permute-start.5 = (bf16[256,1024]{1,0:T(8,128)(2,1)S(1)}, bf16[256,1024]{1,0:T(8,128)(2,1)S(1)}, u32[]{:S(2)}, u32[]{:S(2)}) collective-permute-start(bf16[256,1024]{1,0:T(8,128)(2,1)S(1)} %get-tuple-element.30.own), channel_id=1, source_target_pairs={{0,16},{8,24},{16,0},{24,8},{1,17},{9,25},{17,1},{25,9},{2,18},{10... | collective-permute-start | bytes 1572872 | tf_op jit(solution)/shard_map/ppermute | solution.py:56
  125.9 6.5 %copy-start.15 = (f32[256,1536]{1,0:T(8,128)S(1)}, f32[256,1536]{1,0:T(8,128)}, u32[]{:S(2)}) copy-start(f32[256,1536]{1,0:T(8,128)} %param.28) | copy-start | bytes 4718596
  128.2 20.5 %collective-permute-start.20 = (bf16[256,1536]{1,0:T(8,128)(2,1)S(1)}, bf16[256,1536]{1,0:T(8,128)(2,1)S(1)}, u32[]{:S(2)}, u32[]{:S(2)}) collective-permute-start(bf16[256,1536]{1,0:T(8,128)(2,1)S(1)} %get-tuple-element.24.own), channel_id=1, source_target_pairs={{0,8},{8,0},{16,24},{24,16},{1,9},{9,1},{17,25},{25,17},{2,10},{10... | collective-permute-start | bytes 2359304 | tf_op jit(solution)/shard_map/ppermute | solution.py:56
  128.6 42.6 %collective-permute-start.32 = (bf16[1024,512]{1,0:T(8,128)(2,1)S(1)}, bf16[1024,512]{1,0:T(8,128)(2,1)S(1)}, u32[]{:S(2)}, u32[]{:S(2)}) collective-permute-start(bf16[1024,512]{1,0:T(8,128)(2,1)S(1)} %pad_maximum_fusion.6.own), channel_id=1, source_target_pairs={{0,8},{8,0},{16,24},{24,16},{1,9},{9,1},{17,25},{25,17},{2,10},{10... | collective-permute-start | bytes 3145736 | tf_op jit(solution)/shard_map/ppermute | solution.py:56
  130.4 42.8 %collective-permute-start.33 = (bf16[1024,512]{1,0:T(8,128)(2,1)S(1)}, bf16[1024,512]{1,0:T(8,128)(2,1)S(1)}, u32[]{:S(2)}, u32[]{:S(2)}) collective-permute-start(bf16[1024,512]{1,0:T(8,128)(2,1)S(1)} %pad_maximum_fusion.6.own), channel_id=1, source_target_pairs={{0,16},{8,24},{16,0},{24,8},{1,17},{9,25},{17,1},{25,9},{2,18},{10... | collective-permute-start | bytes 3145736 | tf_op jit(solution)/shard_map/ppermute | solution.py:56
  132.4 41.0 %collective-permute-start.21 = (bf16[256,1536]{1,0:T(8,128)(2,1)S(1)}, bf16[256,1536]{1,0:T(8,128)(2,1)S(1)}, u32[]{:S(2)}, u32[]{:S(2)}) collective-permute-start(bf16[256,1536]{1,0:T(8,128)(2,1)S(1)} %get-tuple-element.24.own), channel_id=1, source_target_pairs={{0,16},{8,24},{16,0},{24,8},{1,17},{9,25},{17,1},{25,9},{2,18},{10... | collective-permute-start | bytes 2359304 | tf_op jit(solution)/shard_map/ppermute | solution.py:56
  134.7 53.3 %collective-permute-start.12 = (bf16[256,1536]{1,0:T(8,128)(2,1)S(1)}, bf16[256,1536]{1,0:T(8,128)(2,1)S(1)}, u32[]{:S(2)}, u32[]{:S(2)}) collective-permute-start(bf16[256,1536]{1,0:T(8,128)(2,1)S(1)} %get-tuple-element.27.own), channel_id=1, source_target_pairs={{0,8},{8,0},{16,24},{24,16},{1,9},{9,1},{17,25},{25,17},{2,10},{10... | collective-permute-start | bytes 2359304 | tf_op jit(solution)/shard_map/ppermute | solution.py:56
  148.7 41.5 %collective-permute-start.13 = (bf16[256,1536]{1,0:T(8,128)(2,1)S(1)}, bf16[256,1536]{1,0:T(8,128)(2,1)S(1)}, u32[]{:S(2)}, u32[]{:S(2)}) collective-permute-start(bf16[256,1536]{1,0:T(8,128)(2,1)S(1)} %get-tuple-element.27.own), channel_id=1, source_target_pairs={{0,16},{8,24},{16,0},{24,8},{1,17},{9,25},{17,1},{25,9},{2,18},{10... | collective-permute-start | bytes 2359304 | tf_op jit(solution)/shard_map/ppermute | solution.py:56
  171.2 35.4 %collective-permute-start.22 = (bf16[128,1536]{1,0:T(8,128)(2,1)S(1)}, bf16[128,1536]{1,0:T(8,128)(2,1)S(1)}, u32[]{:S(2)}, u32[]{:S(2)}) collective-permute-start(bf16[128,1536]{1,0:T(8,128)(2,1)S(1)} %slice.112), channel_id=1, source_target_pairs={{0,16},{8,24},{16,0},{24,8},{1,17},{9,25},{17,1},{25,9},{2,18},{10... | collective-permute-start | bytes 1179656 | tf_op jit(solution)/shard_map/ppermute | solution.py:56
  173.2 31.0 %collective-permute-start.6 = (bf16[128,1024]{1,0:T(8,128)(2,1)S(1)}, bf16[128,1024]{1,0:T(8,128)(2,1)S(1)}, u32[]{:S(2)}, u32[]{:S(2)}) collective-permute-start(bf16[128,1024]{1,0:T(8,128)(2,1)S(1)} %slice.100), channel_id=1, source_target_pairs={{0,16},{8,24},{16,0},{24,8},{1,17},{9,25},{17,1},{25,9},{2,18},{10... | collective-permute-start | bytes 786440 | tf_op jit(solution)/shard_map/ppermute | solution.py:56
  173.3 31.2 %collective-permute-start.7 = (bf16[128,1024]{1,0:T(8,128)(2,1)S(1)}, bf16[128,1024]{1,0:T(8,128)(2,1)S(1)}, u32[]{:S(2)}, u32[]{:S(2)}) collective-permute-start(bf16[128,1024]{1,0:T(8,128)(2,1)S(1)} %slice.101), channel_id=1, source_target_pairs={{0,8},{8,0},{16,24},{24,16},{1,9},{9,1},{17,25},{25,17},{2,10},{10... | collective-permute-start | bytes 786440 | tf_op jit(solution)/shard_map/ppermute | solution.py:56
  188.0 34.4 %collective-permute-start.34 = (bf16[512,512]{1,0:T(8,128)(2,1)S(1)}, bf16[512,512]{1,0:T(8,128)(2,1)S(1)}, u32[]{:S(2)}, u32[]{:S(2)}) collective-permute-start(bf16[512,512]{1,0:T(8,128)(2,1)S(1)} %slice.118), channel_id=1, source_target_pairs={{0,16},{8,24},{16,0},{24,8},{1,17},{9,25},{17,1},{25,9},{2,18},{10... | collective-permute-start | bytes 1572872 | tf_op jit(solution)/shard_map/ppermute | solution.py:56
  190.2 32.3 %collective-permute-start.35 = (bf16[512,512]{1,0:T(8,128)(2,1)S(1)}, bf16[512,512]{1,0:T(8,128)(2,1)S(1)}, u32[]{:S(2)}, u32[]{:S(2)}) collective-permute-start(bf16[512,512]{1,0:T(8,128)(2,1)S(1)} %slice.119), channel_id=1, source_target_pairs={{0,8},{8,0},{16,24},{24,16},{1,9},{9,1},{17,25},{25,17},{2,10},{10... | collective-permute-start | bytes 1572872 | tf_op jit(solution)/shard_map/ppermute | solution.py:56
  204.2 9.9 %collective-permute-start.23 = (bf16[128,1536]{1,0:T(8,128)(2,1)S(1)}, bf16[128,1536]{1,0:T(8,128)(2,1)S(1)}, u32[]{:S(2)}, u32[]{:S(2)}) collective-permute-start(bf16[128,1536]{1,0:T(8,128)(2,1)S(1)} %slice.113), channel_id=1, source_target_pairs={{0,8},{8,0},{16,24},{24,16},{1,9},{9,1},{17,25},{25,17},{2,10},{10... | collective-permute-start | bytes 1179656 | tf_op jit(solution)/shard_map/ppermute | solution.py:56
  204.5 16.1 %collective-permute-start.14 = (bf16[128,1536]{1,0:T(8,128)(2,1)S(1)}, bf16[128,1536]{1,0:T(8,128)(2,1)S(1)}, u32[]{:S(2)}, u32[]{:S(2)}) collective-permute-start(bf16[128,1536]{1,0:T(8,128)(2,1)S(1)} %slice.106), channel_id=1, source_target_pairs={{0,16},{8,24},{16,0},{24,8},{1,17},{9,25},{17,1},{25,9},{2,18},{10... | collective-permute-start | bytes 1179656 | tf_op jit(solution)/shard_map/ppermute | solution.py:56
  206.5 14.1 %collective-permute-start.15 = (bf16[128,1536]{1,0:T(8,128)(2,1)S(1)}, bf16[128,1536]{1,0:T(8,128)(2,1)S(1)}, u32[]{:S(2)}, u32[]{:S(2)}) collective-permute-start(bf16[128,1536]{1,0:T(8,128)(2,1)S(1)} %slice.107), channel_id=1, source_target_pairs={{0,8},{8,0},{16,24},{24,16},{1,9},{9,1},{17,25},{25,17},{2,10},{10... | collective-permute-start | bytes 1179656 | tf_op jit(solution)/shard_map/ppermute | solution.py:56
  (13 other events, 49.3 us)

commit v3 on v2

--- a/solution.py
+++ b/solution.py
@@ -1,3 +1,4 @@
+import functools
 import math
 
 import jax
@@ -177,6 +178,313 @@
     return jnp.where(even, total, other), jnp.where(even, other, total)
 
 
+def fused_kernel(groups, shards, *refs):
+    refs = list(refs)
+
+    def take(n):
+        got, refs[:n] = refs[:n], []
+        return got
+
+    inner, outer, moment = take(3), take(5), take(5)
+    parts, terms, basis = take(2), take(2), take(2)
+    weights, master, momentum = take(5), take(5), take(5)
+    inner_v, outer_v, moment_v = take(3), take(5), take(5)
+    send1, recv1, recv2 = take(3), take(3), take(3)
+    own, by_x, by_y, far = take(5), take(5), take(5), take(5)
+    c_recv1, c_relay, c_recv2, s_send, s_recv = take(5)
+    load_sem, store_sem = take(2)
+    rs1, rs2, c1, c2, sh, agx, agy, agf = [take(2) for _ in range(8)]
+
+    rep, shard = lax.axis_index("rep"), lax.axis_index("shard")
+
+    def remote(src, dst, sems, at, rep_bit, shard_bit=0):
+        return pltpu.make_async_remote_copy(
+            src_ref=src,
+            dst_ref=dst,
+            send_sem=sems[0].at[at],
+            recv_sem=sems[1].at[at],
+            device_id=(rep ^ rep_bit, shard ^ shard_bit),
+            device_id_type=pl.DeviceIdType.MESH,
+        )
+
+    loads = {}
+    for kind, (src, dst) in enumerate(((inner, inner_v), (outer, outer_v), (moment, moment_v))):
+        for m in range(len(src)):
+            loads[kind, m] = pltpu.make_async_copy(src[m], dst[m], load_sem.at[kind, m])
+            loads[kind, m].start()
+
+    barrier = pltpu.get_barrier_semaphore()
+    shard_bits = [1 << i for i in range(shards.bit_length() - 1)]
+    greet = [(1, 0), (2, 0)] + [(0, bit) for bit in shard_bits]
+    for rep_bit, shard_bit in greet:
+        pl.semaphore_signal(
+            barrier,
+            inc=1,
+            device_id=(rep ^ rep_bit, shard ^ shard_bit),
+            device_id_type=pl.DeviceIdType.MESH,
+        )
+    pl.semaphore_wait(barrier, len(greet))
+
+    sends, stores = [], []
+
+    def go(copy):
+        copy.start()
+        sends.append(copy)
+        return copy
+
+    def store(src, dst, kind, m):
+        copy = pltpu.make_async_copy(src, dst, store_sem.at[kind, m])
+        copy.start()
+        stores.append(copy)
+
+    first, second = (1, 2), (2, 1)
+    step = 16
+
+    def sizes(m):
+        rows, width = own[m].shape
+        return rows // 2, width
+
+    def columns(owner, width):
+        return pl.ds(pl.multiple_of(owner * width, 128), width)
+
+    def over_rows(rows, body):
+        def one(i, carry):
+            body(pl.multiple_of(i * step, step))
+            return carry
+
+        lax.fori_loop(0, rows // step, one, 0)
+
+    def phase_a(m):
+        half, width = sizes(m)
+        loads[0, m].wait()
+        out = []
+        for p in range(2):
+            def body(at, p=p):
+                low = pl.ds(pl.multiple_of(p * half + at, step), step)
+                for k, owner in enumerate((rep ^ 3, rep ^ first[p])):
+                    to = pl.ds(pl.multiple_of(k * half + at, step), step)
+                    send1[m][p, to, :] = pack(inner_v[m][low, columns(owner, width)], inner_limit)
+
+            over_rows(half, body)
+            out.append(go(remote(send1[m].at[p], recv1[m].at[p], rs1, (m, p), first[p])))
+        return out
+
+    def phase_b(m, came):
+        half, width = sizes(m)
+        out = []
+        for p in range(2):
+            came[p].wait_recv()
+
+            def body(at, p=p):
+                low = pl.ds(pl.multiple_of(p * half + at, step), step)
+                to = pl.ds(at, step)
+                relay = inner_v[m][low, columns(rep ^ second[p], width)]
+                relay = relay + unpack(recv1[m][p, to, :], inner_limit)
+                recv1[m][p, to, :] = pack(relay, 2 * inner_limit)
+
+            over_rows(half, body)
+            src = recv1[m].at[p, pl.ds(0, half)]
+            out.append(go(remote(src, recv2[m].at[p], rs2, (m, p), second[p])))
+        return out
+
+    def spread(m, p):
+        half, _ = sizes(m)
+        rows = pl.ds(p * half, half)
+        x = go(remote(own[m].at[rows], by_x[m].at[rows], agx, (m, p), 1))
+        y = go(remote(own[m].at[rows], by_y[m].at[rows], agy, (m, p), 2))
+        return x, y
+
+    def update(m, low, delta):
+        outer_now = outer_v[m][low, :]
+        moment_new = decay_moment * moment_v[m][low, :] + delta
+        master_new = outer_now - rate_outer * (delta + decay_moment * moment_new)
+        own[m][low, :] = master_new.astype(jnp.bfloat16)
+        outer_v[m][low, :] = master_new
+        moment_v[m][low, :] = moment_new
+
+    def keep(m):
+        _, width = sizes(m)
+        store(outer_v[m], master[m], 0, m)
+        store(moment_v[m], momentum[m], 1, m)
+        store(own[m], weights[m].at[:, columns(rep, width)], 2, m)
+
+    def phase_c(m, came):
+        half, width = sizes(m)
+        loads[1, m].wait()
+        loads[2, m].wait()
+        out = []
+        for p in range(2):
+            came[p].wait_recv()
+
+            def body(at, p=p):
+                low = pl.ds(pl.multiple_of(p * half + at, step), step)
+                near = pl.ds(pl.multiple_of(half + at, step), step)
+                total = inner_v[m][low, columns(rep, width)]
+                total = total + unpack(recv1[m][p, near, :], inner_limit)
+                total = total + unpack(recv2[m][p, pl.ds(at, step), :], 2 * inner_limit)
+                update(m, low, outer_v[m][low, :] - total * (1.0 / groups))
+
+            over_rows(half, body)
+            out.append(spread(m, p))
+        keep(m)
+        return out
+
+    def forward(m, out):
+        half, _ = sizes(m)
+        top, low = pl.ds(0, half), pl.ds(half, half)
+        out[0][0].wait_recv()
+        a = go(remote(by_x[m].at[top], far[m].at[top], agf, (m, 0), 2))
+        out[1][1].wait_recv()
+        b = go(remote(by_y[m].at[low], far[m].at[low], agf, (m, 1), 1))
+        return a, b
+
+    def finish(m, out, far_out):
+        _, width = sizes(m)
+        out[1][0].wait_recv()
+        store(by_x[m], weights[m].at[:, columns(rep ^ 1, width)], 3, m)
+        out[0][1].wait_recv()
+        store(by_y[m], weights[m].at[:, columns(rep ^ 2, width)], 4, m)
+        far_out[0].wait_recv()
+        far_out[1].wait_recv()
+        store(far[m], weights[m].at[:, columns(rep ^ 3, width)], 5, m)
+
+    thin = terms[0].shape[1]
+
+    def coeff_a():
+        out = []
+        for p in range(2):
+            for k, owner in enumerate((rep ^ 3, rep ^ first[p])):
+                src = parts[p].at[:, columns(owner, thin)]
+                out.append(go(remote(src, c_recv1.at[p, k], c1, (p, k), first[p])))
+        return out
+
+    def coeff_b(came):
+        out = []
+        for p in range(2):
+            came[2 * p].wait_recv()
+            mine = parts[p][:, columns(rep ^ second[p], thin)]
+            c_relay[p] = mine + c_recv1[p, 0]
+            out.append(go(remote(c_relay.at[p], c_recv2.at[p], c2, p, second[p])))
+        return out
+
+    even = shard % 2 == 0
+
+    def hop(slot, bit):
+        return go(remote(s_send.at[slot], s_recv.at[slot], sh, slot, 0, bit))
+
+    def coeff_c(came, later):
+        both = []
+        for p in range(2):
+            came[2 * p + 1].wait_recv()
+            later[p].wait_recv()
+            total = parts[p][:, columns(rep, thin)] + c_recv1[p, 1] + c_recv2[p]
+            both.append(terms[p][...] - total * (1.0 / groups))
+        s_send[0] = jnp.where(even, both[1], both[0])
+        s_send[1] = jnp.where(even, both[0], both[1])
+        return hop(0, 1)
+
+    def coeff_d(slot, came, bit):
+        came.wait_recv()
+        if slot == 1:
+            s_send[1] = s_send[1] + s_recv[0]
+        else:
+            s_send[slot] = s_send[slot - 1] + s_recv[slot - 1]
+        return hop(slot, bit)
+
+    def coeff_f(came):
+        came.wait_recv()
+        last = len(shard_bits)
+        mine, other = s_send[last], s_recv[last]
+        coeffs = (jnp.where(even, mine, other), jnp.where(even, other, mine))
+        outs = []
+        for p, m in ((0, 3), (1, 4)):
+            loads[1, m].wait()
+            loads[2, m].wait()
+            rows = own[m].shape[0]
+            block = math.gcd(rows, 128)
+            coeff = coeffs[p]
+
+            def one(i, carry, p=p, m=m, coeff=coeff, block=block):
+                low = pl.ds(pl.multiple_of(i * block, block), block)
+                update(m, low, rebuild(basis[p][low, :], coeff))
+                return carry
+
+            lax.fori_loop(0, rows // block, one, 0)
+            outs.append([spread(m, 0), spread(m, 1)])
+            keep(m)
+        return outs
+
+    a0 = phase_a(0)
+    ca = coeff_a()
+    a1 = phase_a(1)
+    cb = coeff_b(ca)
+    a2 = phase_a(2)
+    hopped = coeff_c(ca, cb)
+    b0 = phase_b(0, a0)
+    hops = shard_bits[1:] + [1]
+    hopped = coeff_d(1, hopped, hops[0])
+    b1 = phase_b(1, a1)
+    for slot, bit in list(enumerate(hops, 1))[1:-1]:
+        hopped = coeff_d(slot, hopped, bit)
+    g0 = phase_c(0, b0)
+    if len(hops) > 1:
+        hopped = coeff_d(len(hops), hopped, hops[-1])
+    b2 = phase_b(2, a2)
+    g3, g4 = coeff_f(hopped)
+    f0 = forward(0, g0)
+    g1 = phase_c(1, b1)
+    f3 = forward(3, g3)
+    f4 = forward(4, g4)
+    g2 = phase_c(2, b2)
+    f1 = forward(1, g1)
+    finish(0, g0, f0)
+    finish(3, g3, f3)
+    finish(4, g4, f4)
+    f2 = forward(2, g2)
+    finish(1, g1, f1)
+    finish(2, g2, f2)
+    for copy in sends:
+        copy.wait_send()
+    for copy in stores:
+        copy.wait()
+
+
+def fused(inner, outer, moment, parts, terms, basis):
+    groups, shards = lax.axis_size("rep"), lax.axis_size("shard")
+    f32, bf16 = jnp.float32, jnp.bfloat16
+    anywhere = pl.BlockSpec(memory_space=pl.ANY)
+    local = pl.BlockSpec(memory_space=pltpu.VMEM)
+    own = [x.shape for x in outer]
+    code = [(2, x.shape[0], x.shape[1] // groups) for x in inner]
+    half = [(2, x.shape[0] // 2, x.shape[1] // groups) for x in inner]
+    thin = terms[0].shape
+    hops = shards.bit_length()
+    vm, dma = pltpu.VMEM, pltpu.SemaphoreType.DMA
+    scratch = [vm(x.shape, f32) for x in inner]
+    scratch += [vm(x, f32) for x in own + own]
+    scratch += [vm(x, bf16) for x in code + code + half + own * 4]
+    scratch += [vm((2, 2) + thin, f32), vm((2,) + thin, f32), vm((2,) + thin, f32)]
+    scratch += [vm((hops,) + thin, f32), vm((hops,) + thin, f32)]
+    scratch += [dma((3, 5)), dma((6, 5))]
+    for shape in ((3, 2), (3, 2), (2, 2), (2,), (hops,), (5, 2), (5, 2), (5, 2)):
+        scratch += [dma(shape), dma(shape)]
+    wide = [jax.ShapeDtypeStruct((x[0], x[1] * groups), bf16) for x in own]
+    slim = [jax.ShapeDtypeStruct(x, f32) for x in own]
+    return pl.pallas_call(
+        functools.partial(fused_kernel, groups, shards),
+        out_shape=wide + slim + slim,
+        in_specs=[anywhere] * 13 + [local] * 6,
+        out_specs=[anywhere] * 15,
+        scratch_shapes=scratch,
+        compiler_params=pltpu.CompilerParams(
+            collective_id=0, has_side_effects=True, vmem_limit_bytes=60 * 2**20
+        ),
+        cost_estimate=pl.CostEstimate(
+            flops=10**9, bytes_accessed=60 * 2**20, transcendentals=10**7
+        ),
+    )(*inner, *outer, *moment, *parts, *terms, *basis)
+
+
 def on_device(
     inner_wqkv,
     inner_w1,
@@ -196,6 +504,16 @@
     basis_wo,
     basis_w2,
 ):
+    shards = lax.axis_size("shard")
+    if lax.axis_size("rep") == 4 and shards > 1 and not shards & (shards - 1):
+        return fused(
+            (inner_wqkv[0], inner_w1[0], inner_w3[0]),
+            (outer_wqkv, outer_w1, outer_w3, outer_wo, outer_w2),
+            (moment_wqkv, moment_w1, moment_w3, moment_wo, moment_w2),
+            (project(basis_wo, inner_wo[0]), project(basis_w2, inner_w2[0])),
+            (project(basis_wo, outer_wo), project(basis_w2, outer_w2)),
+            (basis_wo, basis_w2),
+        )
     groups = lax.axis_size("rep")
     d_qkv = outer_wqkv - sum_columns(inner_wqkv[0]) / groups
     coeff_out, coeff_down = coefficients(

time: 227 us -> 232 us (1.022)
  Pallas kernels: 8.7 us -> 187 us
  waiting for transfers between devices: 125 us -> 0 us
  starting transfers between devices: 40.1 us -> 0 us
  other arithmetic: 27.6 us -> 0 us
  local copies, waits for them, and re-layouts: 8.69 us -> 28.5 us
    pallas_call x5 -> x1, Pallas kernels: 8.7 us -> 187 us  [fused(): pl.pallas_call(functools.partial(fused_kernel, groups, shards), out_shape...]
    ppermute x36 -> x0, waiting for transfers between devices: 125 us -> none  [swap(): lax.ppermute(value, axis, [(i, i ^ bit) for i in range(lax.axis_size(axis...]
    ppermute x36 -> x0, starting transfers between devices: 40.1 us -> none  [swap(): lax.ppermute(value, axis, [(i, i ^ bit) for i in range(lax.axis_size(axis...]
    unnamed x50 -> x53, local copies, waits for them, and re-layouts: 1.7 us -> 28.5 us
    convert_element_type x12 -> x0, other arithmetic: 17.9 us -> none  [the longest x9 11.7 us: pack(): return jnp.where(value < 0, -size, size).astype(jnp.bfloat16)]
    add x7 -> x0, other arithmetic: 7.01 us -> none  [the longest x2 5.09 us: scatter_pairs(): block(me) + decode(near, inner_limit) + decode(across, 2 * inner_limit)]
    dynamic_slice x5 -> x0, local copies, waits for them, and re-layouts: 6.78 us -> none  [block(): return lax.dynamic_slice(matrix, (low, owner * width), (rows, width))]
    dot_general x2 -> x0, matrix products: 5.38 us -> none  [rebuild(): jnp.dot(basis, coeff, precision=lax.Precision.HIGHEST, preferred_element_...]
  transfers between devices with their start and end apart: 36 -> 0, of which waited for: 14 -> 0; matrix products, arithmetic and copies ran while one was open for 21% -> 0% of each run, Pallas kernels for 2% -> 0%
where the time goes in v3:
time: 232 us
  Pallas kernels  187 us (81%)
  local copies, waits for them, and re-layouts  28.5 us (12%)
  matrix products  15.2 us (7%)
    pallas_call x1, Pallas kernels, fused(): pl.pallas_call(functools.partial(fused_kernel, groups, shards), out_shape...  187 us
    unnamed x53, local copies, waits for them, and re-layouts  28.5 us
    dot_general x4, matrix products, project(): lax.dot_general(basis, matrix, (((0,), (0,)), ((), ())), precision=lax.Pr...  15.2 us

profile of v3, /device:TPU:0, one launch (start us, length us, event | category | flops | bytes accessed | tf_op | source)
XLA Modules:
  0.0 231.9 jit_solution(15652092856137876835)
XLA Ops:
  0.6 0.0 copy-start
  0.7 0.0 copy-start.5
  0.7 0.0 copy-start.15
  0.7 2.4 %fusion.4.refs_15_ = f32[64,512]{1,0:T(8,128)} fusion(f32[256,64]{0,1:T(8,128)} %param.32, f32[256,512]{1,0:T(8,128)} %refs_6_.1), kind=kOutput, calls=%fused_computation.4 | convolution fusion | flops 100663296 | bytes 720896 | tf_op jit(solution)/shard_map/dot_general | solution.py:18
  3.0 3.2 %fusion.5.refs_16_ = f32[64,512]{1,0:T(8,128)} fusion(f32[768,64]{0,1:T(8,128)} %param.33, f32[768,512]{1,0:T(8,128)} %refs_7_.1), kind=kOutput, calls=%fused_computation.5 | convolution fusion | flops 301989888 | bytes 1900544 | tf_op jit(solution)/shard_map/dot_general | solution.py:18
  6.3 0.0 copy-done.15
  6.3 0.8 copy.32.refs_17_
  7.0 0.0 copy-done.5
  7.0 0.9 copy.33.refs_18_
  8.0 0.0 copy-done
  8.0 2.2 fusion.2.refs_13_
  10.1 7.5 %fusion.refs_14_ = f32[64,2048]{1,0:T(8,128)} fusion(f32[768,64]{0,1:T(8,128)S(1)} %copy-done.5, f32[1,768,2048]{2,1,0:T(8,128)} %param.21), kind=kOutput, calls=%fused_computation | convolution fusion | flops 1207959552 | bytes 7012352 | tf_op jit(solution)/shard_map/dot_general | solution.py:18
  17.6 187.5 %shard_map.280 = (bf16[256,4096]{1,0:T(8,128)(2,1)}, bf16[256,6144]{1,0:T(8,128)(2,1)}, bf16[256,6144]{1,0:T(8,128)(2,1)}, bf16[256,2048]{1,0:T(8,128)(2,1)}, bf...) custom-call(f32[256,4096]{1,0:T(8,128)} %bitcast.17, ...), custom_call_target="tpu_custom_call" | custom-call | flops 1000000000 | bytes 62914560 | tf_op jit(solution)/shard_map/pallas_call | solution.py:473
  205.1 0.0 copy-start.4
  205.1 3.3 %copy.49 = bf16[256,4096]{1,0:T(8,128)(2,1)} copy(bf16[256,4096]{1,0:T(8,128)(2,1)} %get-tuple-element.30) | data formatting | bytes 4194304
  208.4 0.0 copy-done.4
  208.4 0.0 copy-start.3
  208.4 1.7 copy.50
  210.0 1.4 copy-done.3
  211.4 0.0 copy-start.2
  211.4 1.7 copy.51
  213.1 0.3 copy-done.14
  213.4 1.0 copy.52
  214.3 0.8 copy-done.2
  215.1 0.0 copy-start.13
  215.1 1.7 copy.53
  216.8 0.3 copy-done.13
  217.1 0.0 copy-start.11
  217.1 1.0 copy.54
  218.1 0.8 copy-done.11
  218.9 1.1 copy.55
  220.0 0.8 copy-done.10
  220.9 1.1 copy.56
  222.0 0.2 copy-done.17
  222.2 0.8 copy.57
  223.0 0.0 copy-done.9
  223.0 1.1 copy.58
  224.2 0.6 copy-done.12
  224.8 1.0 copy.59
  225.8 0.8 copy-done.8
  226.6 1.1 copy.60
  227.7 0.8 copy-done.7
  228.6 1.1 copy.61
  229.7 0.2 copy-done.16
  229.9 0.8 copy.62
  230.7 0.0 copy-done.6
  230.7 1.1 copy.63
  231.9 0.0 copy-done.1
  (10 shorter events, 0.0 us)
Async XLA Ops:
  0.6 7.3 %copy-start = (f32[1,256,2048]{2,1,0:T(8,128)S(1)}, f32[1,256,2048]{2,1,0:T(8,128)}, u32[]{:S(2)}) copy-start(f32[1,256,2048]{2,1,0:T(8,128)} %param.20) | copy-start | bytes 6291460
  0.7 6.4 %copy-start.5 = (f32[768,64]{0,1:T(8,128)S(1)}, f32[768,64]{0,1:T(8,128)}, u32[]{:S(2)}) copy-start(f32[768,64]{0,1:T(8,128)} %param.33) | copy-start | bytes 589828
  0.7 5.6 %copy-start.15 = (f32[256,64]{0,1:T(8,128)S(1)}, f32[256,64]{0,1:T(8,128)}, u32[]{:S(2)}) copy-start(f32[256,64]{0,1:T(8,128)} %param.32) | copy-start | bytes 196612
  205.1 3.3 %copy-start.4 = (bf16[256,6144]{1,0:T(8,128)(2,1)S(1)}, bf16[256,6144]{1,0:T(8,128)(2,1)}, u32[]{:S(2)}) copy-start(bf16[256,6144]{1,0:T(8,128)(2,1)} %get-tuple-element.31) | copy-start | bytes 9437188
  208.4 3.0 %copy-start.3 = (bf16[256,6144]{1,0:T(8,128)(2,1)S(1)}, bf16[256,6144]{1,0:T(8,128)(2,1)}, u32[]{:S(2)}) copy-start(bf16[256,6144]{1,0:T(8,128)(2,1)} %get-tuple-element.32) | copy-start | bytes 9437188
  211.4 2.0 copy-start.14
  211.4 3.7 %copy-start.2 = (bf16[768,2048]{1,0:T(8,128)(2,1)S(1)}, bf16[768,2048]{1,0:T(8,128)(2,1)}, u32[]{:S(2)}) copy-start(bf16[768,2048]{1,0:T(8,128)(2,1)} %get-tuple-element.34) | copy-start | bytes 9437188
  215.1 2.0 copy-start.13
  217.1 1.8 copy-start.11
  218.9 2.0 copy-start.10
  220.8 1.4 copy-start.17
  220.8 2.2 copy-start.9
  223.0 1.8 copy-start.12
  224.8 1.8 copy-start.8
  226.6 2.0 copy-start.7
  228.6 1.4 copy-start.16
  228.6 2.2 copy-start.6
  229.9 1.9 copy-start.1
